TPU v7x, 256 devices: a whole 4x4x8 slice. The times are simulated.
256 devices in a mesh: rep: 16 (over z_hi, x, core), tp: 16 (over y, z_lo).
Axes of the slice: x: 4, y: 4, z: 8 (z_hi: 2, z_lo: 4; z = z_hi * 4 + z_lo), core: 2. Of those that a mesh axis runs over, the one named last changes fastest.
Arguments:
- trainer_weight: bfloat16 [32, 512, 256], P('rep', 'tp'), may hold values from -0.25 to 0.25
- bucket_slot: int32 [32], replicated, may hold values from 0 to 31, each once
- bucket_version: int32 [32], replicated, may hold values from 0 to 2
- replica_version: int32 [16, 32], P('rep'), may hold values from 0 to 2
- old_weight: bfloat16 [16, 512, 8192], P('rep', None, 'tp'), may hold values from -1 to 1
- old_scale: float32 [16, 4, 64], P('rep', None, 'tp'), may hold values from 0.08 to 0.3
- q_nope: bfloat16 [2, 16, 256, 4096], P(None, 'rep', None, 'tp'), may hold values from -6 to 6
- q_rope: bfloat16 [2, 16, 256, 2048], P(None, 'rep', None, 'tp'), may hold values from -80 to 80
- cache_latent: bfloat16 [16, 256, 384, 512], P('rep', 'tp'), may hold values from -6 to 6
- cache_rope: bfloat16 [16, 256, 24576], P('rep', 'tp'), may hold values from -16 to 16
- new_token: bfloat16 [2, 16, 256, 576], P(None, 'rep', 'tp'), may hold values from -6 to 6
- lengths: int32 [16, 256], P('rep', 'tp'), may hold values from 2 to 384, as said below
- out_weight: bfloat16 [4096, 7168], P('tp'), may hold values from -0.09375 to 0.09375
Outputs:
- served_weight: bfloat16 [16, 512, 8192], P('rep', None, 'tp')
- served_scale: float32 [16, 4, 64], P('rep', None, 'tp')
- decoded: bfloat16 [2, 16, 256, 7168], P(None, 'rep', 'tp')
Inputs may be any that keep to these rules, and one draw needn't show every extreme that they name: `bucket_slot`: each slot holds exactly one head's bucket; slot k lies on rep index k // (32 / 16). `lengths`: every replica has a row of length 384.
All inputs are finite; a program needn't handle non-finite values. Where the computation divides by a largest or mean magnitude, that divisor is 1e-20 or more.
Results may differ from a plain program's by a relative error of at most 0.027.
Values may be sent and summed in bfloat16 or wider, within the bound.
A program may use at most 128 MiB of HBM per device.

v0:
```python
import jax
import jax.numpy as jnp
from jax import lax
from jax.sharding import PartitionSpec as P

HEADS = 32
LAT = 512
NOPE = 128
ROPE = 64
VDIM = 128
BLOCK = 128
STEPS = 2


EPSILON = 1e-06


def attend(row_lat, row_rope, keys_lat, keys_rope, fresh_tok, lengths, step_idx):
    fresh_lat = fresh_tok[:, :, :LAT]
    fresh_rope = fresh_tok[:, :, LAT:]
    scaling = (NOPE + ROPE) ** (-0.5)
    cached = jnp.einsum(
        "rhl,rjl->rhj", row_lat, keys_lat, preferred_element_type=jnp.float32
    ) + jnp.einsum("rhe,rje->rhj", row_rope, keys_rope, preferred_element_type=jnp.float32)
    newest = jnp.einsum(
        "rhl,rtl->rht", row_lat, fresh_lat, preferred_element_type=jnp.float32
    ) + jnp.einsum("rhe,rte->rht", row_rope, fresh_rope, preferred_element_type=jnp.float32)
    scores = jnp.concatenate([cached, newest], axis=2) * scaling
    positions = keys_lat.shape[1]
    usable_cache = jnp.arange(positions, dtype=jnp.int32)[None, :] < lengths[:, None]
    usable_new = jnp.broadcast_to(
        (jnp.arange(STEPS, dtype=jnp.int32) <= step_idx)[None, :], (keys_lat.shape[0], STEPS)
    )
    usable = jnp.concatenate([usable_cache, usable_new], axis=1)[:, None, :]
    scores = jnp.where(usable, scores, -jnp.inf)
    row_max = jnp.max(scores, axis=2, keepdims=True)
    expped = jnp.exp(scores - row_max)
    weights_bf = (expped / jnp.sum(expped, axis=2, keepdims=True)).astype(jnp.bfloat16)
    attended = jnp.einsum(
        "rhj,rjl->rhl", weights_bf[:, :, :positions], keys_lat, preferred_element_type=jnp.float32
    ) + jnp.einsum(
        "rht,rtl->rhl", weights_bf[:, :, positions:], fresh_lat, preferred_element_type=jnp.float32
    )
    return attended.astype(jnp.bfloat16)


def local(
    trainer_weight,
    bucket_slot,
    bucket_version,
    replica_version,
    old_weight,
    old_scale,
    q_nope,
    q_rope,
    cache_latent,
    cache_rope,
    new_token,
    lengths,
    out_weight,
):
    n_tp = lax.axis_size("tp")
    tp_pos = lax.axis_index("tp")
    slots_dev, rows_dev, columns = trainer_weight.shape
    lat_blocks = LAT // BLOCK
    heads_dev = HEADS // n_tp
    own_rows = trainer_weight.astype(jnp.float32).reshape(slots_dev, rows_dev, 2, BLOCK)
    row_peak = jnp.max(jnp.abs(own_rows), axis=3)
    row_block = (tp_pos * rows_dev + jnp.arange(rows_dev, dtype=jnp.int32)) // BLOCK
    member = row_block[:, None] == jnp.arange(lat_blocks, dtype=jnp.int32)[None, :]
    own_peak = jnp.max(jnp.where(member[None, :, :, None], row_peak[:, :, None, :], 0.0), axis=1)
    block_peak = lax.pmax(own_peak, "tp")
    scales = block_peak + EPSILON
    row_scale = jnp.sum(jnp.where(member[None, :, :, None], scales[:, None, :, :], 0.0), axis=2)
    payload = (
        (own_rows / row_scale[..., None]).astype(jnp.bfloat16).reshape(slots_dev, rows_dev, columns)
    )
    bundle = (payload, scales)
    pushed = (
        lax.all_gather(bundle[0], "rep", axis=0, tiled=True),
        lax.all_gather(bundle[1].astype(jnp.bfloat16), "rep", axis=0, tiled=True).astype(
            jnp.float32
        ),
    )
    arranged = tuple((jnp.take(entire, bucket_slot, axis=0) for entire in pushed))
    resharded = lax.all_to_all(arranged[0], "tp", split_axis=0, concat_axis=1, tiled=True)
    head_first = tp_pos * heads_dev
    new_scale = lax.dynamic_slice_in_dim(arranged[1], head_first, heads_dev, 0)
    mine_tags = lax.dynamic_slice_in_dim(bucket_version, head_first, heads_dev, 0)
    mine_held = lax.dynamic_slice_in_dim(replica_version[0], head_first, heads_dev, 0)
    stale = mine_held != mine_tags
    served = jnp.where(
        stale[None, :, None],
        jnp.transpose(resharded, (1, 0, 2)),
        old_weight[0].reshape(LAT, heads_dev, columns),
    )
    served_blocks = jnp.where(
        stale[None, :, None],
        jnp.transpose(new_scale, (1, 0, 2)),
        old_scale[0].reshape(lat_blocks, heads_dev, 2),
    )
    served_weight = served.reshape(1, LAT, heads_dev * columns)
    served_scale = served_blocks.reshape(1, lat_blocks, heads_dev * 2)
    dequant = (
        served.astype(jnp.float32).reshape(lat_blocks, BLOCK, heads_dev, 2, BLOCK)
        * served_blocks.reshape(lat_blocks, 1, heads_dev, 2, 1)
    ).astype(jnp.bfloat16)
    dequant = dequant.reshape(LAT, heads_dev, 2, BLOCK)
    key_map = dequant[:, :, 0, :]
    value_map = dequant[:, :, 1, :]
    rows_total = q_nope.shape[2]
    rows_here = cache_latent.shape[1]
    fresh_tok = jnp.transpose(new_token[:, 0], (1, 0, 2))
    keys_rope = cache_rope[0].reshape(rows_here, -1, ROPE)
    decoded_steps = []
    for step_idx in range(STEPS):
        query_nope = q_nope[step_idx, 0].reshape(rows_total, heads_dev, NOPE)
        query_lat = jnp.einsum(
            "rhn,lhn->rhl", query_nope, key_map, preferred_element_type=jnp.float32
        ).astype(jnp.bfloat16)
        query_rope = q_rope[step_idx, 0].reshape(rows_total, heads_dev, ROPE)
        row_lat, row_rope = (
            lax.all_to_all(query_lat, "tp", split_axis=0, concat_axis=1, tiled=True),
            lax.all_to_all(query_rope, "tp", split_axis=0, concat_axis=1, tiled=True),
        )
        attended = attend(
            row_lat, row_rope, cache_latent[0], keys_rope, fresh_tok, lengths[0], step_idx
        )
        head_lat = lax.all_to_all(attended, "tp", split_axis=1, concat_axis=0, tiled=True)
        heads_out = jnp.einsum(
            "rhl,lhv->rhv", head_lat, value_map, preferred_element_type=jnp.float32
        ).astype(jnp.bfloat16)
        heads_out = heads_out.reshape(rows_total, heads_dev * VDIM)

        def projected(start, count, source=heads_out):
            return jnp.dot(source, out_weight, preferred_element_type=jnp.float32)

        summed = lax.psum_scatter(
            projected(jnp.int32(0), rows_here * lax.axis_size("tp")).astype(jnp.bfloat16),
            "tp",
            scatter_dimension=0,
            tiled=True,
        )
        decoded_steps.append(summed)
    decoded = jnp.stack(decoded_steps)[:, None]
    return (served_weight, served_scale, decoded)


def solution(mesh):
    return jax.shard_map(
        local,
        mesh=mesh,
        in_specs=(
            P("rep", "tp", None),
            P(),
            P(),
            P("rep", None),
            P("rep", None, "tp"),
            P("rep", None, "tp"),
            P(None, "rep", None, "tp"),
            P(None, "rep", None, "tp"),
            P("rep", "tp", None, None),
            P("rep", "tp", None),
            P(None, "rep", "tp", None),
            P("rep", "tp"),
            P("tp", None),
        ),
        out_specs=(P("rep", None, "tp"), P("rep", None, "tp"), P(None, "rep", "tp", None)),
        check_vma=False,
    )
```

profile of v0, /device:TPU:4, one launch (start us, length us, event | category | flops | bytes accessed | tf_op | source)
XLA Modules:
  0.0 413.1 jit_solution(6630919878538907747)
XLA Ops:
  9.8 45.0 %pmax.7 = f32[2,4,2]{1,2,0:T(2,128)S(1)} all-reduce(f32[2,4,2]{1,2,0:T(2,128)S(1)} %select_reduce_fusion.1), channel_id=1, replica_groups=mesh['rep'=16,'tp'=16] {'tp'}, use_global_device_ids=true, to_apply=%region_2.3 | all-reduce | flops 16 | bytes 128 | tf_op jit(solution)/shard_map/pmax | solution.py:72
  56.0 25.0 %all_gather.6 = bf16[32,32,256]{2,1,0:T(8,128)(2,1)S(1)} all-gather(bf16[2,32,256]{2,1,0:T(8,128)(2,1)S(1)} %fusion.34), channel_id=1, replica_groups=mesh['rep'=16,'tp'=16] {'rep'}, dimensions={0}, use_global_device_ids=true | all-gather | bytes 557056 | tf_op jit(solution)/shard_map/all_gather | solution.py:80
  81.6 0.9 broadcast_select_fusion
  82.5 3.6 all-to-all-start
  86.2 31.1 %all_gather.7 = bf16[32,4,2]{1,2,0:T(2,128)(2,1)S(1)} all-gather(bf16[2,4,2]{1,2,0:T(2,128)(2,1)S(1)} %get-tuple-element.33), channel_id=1, replica_groups=mesh['rep'=16,'tp'=16] {'rep'}, dimensions={0}, use_global_device_ids=true | all-gather | bytes 544 | tf_op jit(solution)/shard_map/all_gather | solution.py:81
  120.5 7.4 %all-to-all-start.2 = ((bf16[16,2,1024]{2,1,0:T(2,128)(2,1)}), bf16[16,2,1024]{2,1,0:T(2,128)(2,1)S(1)}, u32[]{:S(2)}, u32[]{:S(2)}) async-start(bf16[16,2,1024]{2,1,0:T(2,128)(2,1)} %reshape.129), calls=%async_computation.2 | async-start | bytes 131072 | tf_op jit(solution)/shard_map/all_to_all | solution.py:124
  129.2 1.2 copy.293
  130.4 5.6 %all-to-all-done.2 = bf16[16,2,1024]{2,1,0:T(2,128)(2,1)S(1)} async-done(((bf16[16,2,1024]{2,1,0:T(2,128)(2,1)}), bf16[16,2,1024]{2,1,0:T(2,128)(2,1)S(1)}, u32[]{:S(2)}, u32[]{:S(2)}) %all-to-all-start.2) | async-done | bytes 65568 | tf_op jit(solution)/shard_map/all_to_all | solution.py:124
  136.0 3.6 all-to-all-start.1
  139.7 3.4 reshape_squeeze.25
  143.7 11.7 %all-to-all-done.1 = bf16[256,2,512]{2,1,0:T(2,128)(2,1)S(1)} async-done(((bf16[256,2,512]{2,1,0:T(2,128)(2,1)}), bf16[256,2,512]{2,1,0:T(2,128)(2,1)S(1)}, u32[]{:S(2)}, u32[]{:S(2)}) %all-to-all-start.1) | async-done | bytes 524320 | tf_op jit(solution)/shard_map/all_to_all | solution.py:123
  157.0 0.9 copy.304
  157.9 5.0 %fusion.8 = f32[16,32,384]{2,1,0:T(8,128)S(1)} fusion(bf16[16,32,512]{2,1,0:T(8,128)(2,1)} %copy-done.4, bf16[1,16,384,512]{3,2,1,0:T(8,128)(2,1)} %param.21), kind=kOutput, calls=%fused_computation.12 | convolution fusion | flops 201326592 | bytes 7602176 | tf_op jit(solution)/shard_map/rhl,rjl->rhj/dot_general | solution.py:22
  163.6 3.0 fusion.55
  166.8 1.2 fusion.6
  168.5 18.8 %all_to_all.126 = bf16[16,32,512]{2,0,1:T(8,128)(2,1)S(1)} all-to-all(bf16[16,32,512]{2,0,1:T(8,128)(2,1)S(1)} %copy.306), channel_id=1, replica_groups=mesh['rep'=16,'tp'=16] {'tp'}, dimensions={1} | all-to-all | bytes 1048576 | tf_op jit(solution)/shard_map/all_to_all | solution.py:129
  187.7 2.9 convolution_convert_fusion.1
  192.5 3.5 all-to-all-start.5
  196.4 1.2 copy.311
  197.6 6.5 %all-to-all-done.5 = bf16[16,2,1024]{2,1,0:T(2,128)(2,1)S(1)} async-done(((bf16[16,2,1024]{2,1,0:T(2,128)(2,1)}), bf16[16,2,1024]{2,1,0:T(2,128)(2,1)S(1)}, u32[]{:S(2)}, u32[]{:S(2)}) %all-to-all-start.5) | async-done | bytes 65568 | tf_op jit(solution)/shard_map/all_to_all | solution.py:124
  204.1 3.6 all-to-all-start.4
  208.4 29.7 %all-to-all-done.4 = bf16[256,2,512]{2,1,0:T(2,128)(2,1)S(1)} async-done(((bf16[256,2,512]{2,1,0:T(2,128)(2,1)}), bf16[256,2,512]{2,1,0:T(2,128)(2,1)S(1)}, u32[]{:S(2)}, u32[]{:S(2)}) %all-to-all-start.4) | async-done | bytes 524320 | tf_op jit(solution)/shard_map/all_to_all | solution.py:123
  239.7 0.9 copy.321
  240.5 5.1 %fusion.4 = f32[16,32,384]{2,1,0:T(8,128)S(1)} fusion(bf16[16,32,512]{2,1,0:T(8,128)(2,1)} %copy-done.5, bf16[1,16,384,512]{3,2,1,0:T(8,128)(2,1)} %param.21), kind=kOutput, calls=%fused_computation.8 | convolution fusion | flops 201326592 | bytes 7602176 | tf_op jit(solution)/shard_map/rhl,rjl->rhj/dot_general | solution.py:22
  246.3 3.0 fusion.54
  249.5 1.2 fusion.2
  251.2 31.8 %all_to_all.127 = bf16[16,32,512]{2,0,1:T(8,128)(2,1)S(1)} all-to-all(bf16[16,32,512]{2,0,1:T(8,128)(2,1)S(1)} %copy.323), channel_id=1, replica_groups=mesh['rep'=16,'tp'=16] {'tp'}, dimensions={1} | all-to-all | bytes 1048576 | tf_op jit(solution)/shard_map/all_to_all | solution.py:129
  283.4 3.0 convolution_convert_fusion
  288.0 1.0 copy.326
  289.0 16.0 %reduce-scatter.3.cloned.1.call-done = bf16[16,7168]{1,0:T(8,128)(2,1)} async-done(((bf16[256,7168]{1,0:T(8,128)(2,1)}), bf16[16,7168]{1,0:T(8,128)(2,1)}) %reduce-scatter.3.cloned.1.call-update) | async-done | bytes 229392 | tf_op jit(solution)/shard_map/reduce_scatter | solution.py:138
  305.0 99.4 %reduce-scatter.5.cloned.1.call-done = bf16[16,7168]{1,0:T(8,128)(2,1)} async-done(((bf16[256,7168]{1,0:T(8,128)(2,1)}), bf16[16,7168]{1,0:T(8,128)(2,1)}) %reduce-scatter.5.cloned.1.call-update) | async-done | bytes 229392 | tf_op jit(solution)/shard_map/reduce_scatter | solution.py:138
  404.4 1.9 maximum_bitcast_fusion
  (137 shorter events, 20.6 us)
Async XLA Ops:
  7.2 79.0 %copy-start.15 = (f32[1,4,4]{2,1,0:T(4,128)S(1)}, f32[1,4,4]{2,1,0:T(4,128)}, u32[]{:S(2)}) copy-start(f32[1,4,4]{2,1,0:T(4,128)} %param.18) | copy-start | bytes 196
  7.2 110.8 %copy-start.17 = (s32[1,32]{1,0:T(1,128)S(1)}, s32[1,32]{1,0:T(1,128)}, u32[]{:S(2)}) copy-start(s32[1,32]{1,0:T(1,128)} %param.16) | copy-start | bytes 388
  7.2 110.8 %copy-start.16 = (s32[32]{0:T(128)S(1)}, s32[32]{0:T(128)}, u32[]{:S(2)}) copy-start(s32[32]{0:T(128)} %param.15) | copy-start | bytes 388
  7.2 111.1 %copy-start.11 = (bf16[2,1,256,128]{3,2,1,0:T(8,128)(2,1)S(1)}, bf16[2,1,256,128]{3,2,1,0:T(8,128)(2,1)}, u32[]{:S(2)}) copy-start(bf16[2,1,256,128]{3,2,1,0:T(8,128)(2,1)} %param.20) | copy-start | bytes 393220
  7.2 112.7 %copy-start.7 = (bf16[2,1,256,256]{3,2,1,0:T(8,128)(2,1)S(1)}, bf16[2,1,256,256]{3,2,1,0:T(8,128)(2,1)}, u32[]{:S(2)}) copy-start(bf16[2,1,256,256]{3,2,1,0:T(8,128)(2,1)} %param.19) | copy-start | bytes 786436
  7.2 112.8 %copy-start.6 = (bf16[1,512,512]{2,1,0:T(8,128)(2,1)S(1)}, bf16[1,512,512]{2,1,0:T(8,128)(2,1)}, u32[]{:S(2)}) copy-start(bf16[1,512,512]{2,1,0:T(8,128)(2,1)} %param.17) | copy-start | bytes 1572868
  82.5 38.0 %all-to-all-start = ((bf16[32,32,256]{2,1,0:T(8,128)(2,1)}), bf16[32,32,256]{2,1,0:T(8,128)(2,1)S(1)}, u32[]{:S(2)}, u32[]{:S(2)}) async-start(bf16[32,32,256]{2,1,0:T(8,128)(2,1)} %broadcast_select_fusion), calls=%async_computation | async-start | bytes 1048576 | tf_op jit(solution)/shard_map/all_to_all | solution.py:86
  118.2 1.8 copy-start.13
  120.5 15.5 %all-to-all-start.2 = ((bf16[16,2,1024]{2,1,0:T(2,128)(2,1)}), bf16[16,2,1024]{2,1,0:T(2,128)(2,1)S(1)}, u32[]{:S(2)}, u32[]{:S(2)}) async-start(bf16[16,2,1024]{2,1,0:T(2,128)(2,1)} %reshape.129), calls=%async_computation.2 | async-start | bytes 131072 | tf_op jit(solution)/shard_map/all_to_all | solution.py:124
  128.2 11.4 %copy-start.12 = (bf16[2,1,16,576]{3,2,1,0:T(8,128)(2,1)S(1)}, bf16[2,1,16,576]{3,2,1,0:T(8,128)(2,1)}, u32[]{:S(2)}) copy-start(bf16[2,1,16,576]{3,2,1,0:T(8,128)(2,1)} %param.23) | copy-start | bytes 110596
  128.6 14.6 %copy-start.18 = (s32[1,16]{1,0:T(1,128)S(1)}, s32[1,16]{1,0:T(1,128)}, u32[]{:S(2)}) copy-start(s32[1,16]{1,0:T(1,128)} %param.24) | copy-start | bytes 196
  136.0 19.4 %all-to-all-start.1 = ((bf16[256,2,512]{2,1,0:T(2,128)(2,1)}), bf16[256,2,512]{2,1,0:T(2,128)(2,1)S(1)}, u32[]{:S(2)}, u32[]{:S(2)}) async-start(bf16[256,2,512]{2,1,0:T(2,128)(2,1)} %copy.293), calls=%async_computation.1 | async-start | bytes 1048576 | tf_op jit(solution)/shard_map/all_to_all | solution.py:123
  139.6 165.4 %reduce-scatter.3.cloned.1.call-start = ((), (), s32[]{:S(2)}) async-start(), calls=%async_computation.9 | async-start | bytes 3899392 | tf_op jit(solution)/shard_map/reduce_scatter | solution.py:138
  156.2 0.8 copy-start.4
  157.0 9.8 %slice-start = ((s8[6291456]{0:T(1024)(128)(4,1)}), s8[2097152]{0:T(1024)(128)(4,1)S(1)}, s32[]{:S(2)}) async-start(s8[6291456]{0:T(1024)(128)(4,1)} %bitcast.103), calls=%async_computation.11 | async-start | bytes 4194304
  157.9 5.0 %copy-start.2 = (bf16[16,384,64]{2,1,0:T(8,128)(2,1)S(1)}, bf16[16,384,64]{2,1,0:T(8,128)(2,1)}, u32[]{:S(2)}) copy-start(bf16[16,384,64]{2,1,0:T(8,128)(2,1)} %reshape_squeeze.25) | copy-start | bytes 2359300
  157.9 5.7 %copy-start.9 = (f32[16,32,2]{2,1,0:T(8,128)S(1)}, f32[16,32,2]{2,1,0:T(8,128)}, u32[]{:S(2)}) copy-start(f32[16,32,2]{2,1,0:T(8,128)} %copy.304) | copy-start | bytes 12292
  157.9 8.9 %slice-start.1 = ((s8[6291456]{0:T(1024)(128)(4,1)}), s8[4194304]{0:T(1024)(128)(4,1)S(1)}, s32[]{:S(2)}) async-start(s8[6291456]{0:T(1024)(128)(4,1)} %bitcast.103), calls=%async_computation.12 | async-start | bytes 8388608
  168.0 19.8 %copy-start = (bf16[256,7168]{1,0:T(8,128)(2,1)S(1)}, bf16[256,7168]{1,0:T(8,128)(2,1)}, u32[]{:S(2)}) copy-start(bf16[256,7168]{1,0:T(8,128)(2,1)} %param.25) | copy-start | bytes 11010052
  190.6 0.8 copy-start.10
  192.5 11.6 %all-to-all-start.5 = ((bf16[16,2,1024]{2,1,0:T(2,128)(2,1)}), bf16[16,2,1024]{2,1,0:T(2,128)(2,1)S(1)}, u32[]{:S(2)}, u32[]{:S(2)}) async-start(bf16[16,2,1024]{2,1,0:T(2,128)(2,1)} %reshape.127), calls=%async_computation.6 | async-start | bytes 131072 | tf_op jit(solution)/shard_map/all_to_all | solution.py:124
  204.1 34.0 %all-to-all-start.4 = ((bf16[256,2,512]{2,1,0:T(2,128)(2,1)}), bf16[256,2,512]{2,1,0:T(2,128)(2,1)S(1)}, u32[]{:S(2)}, u32[]{:S(2)}) async-start(bf16[256,2,512]{2,1,0:T(2,128)(2,1)} %copy.311), calls=%async_computation.5 | async-start | bytes 1048576 | tf_op jit(solution)/shard_map/all_to_all | solution.py:123
  207.7 196.7 %reduce-scatter.5.cloned.1.call-start = ((), (), s32[]{:S(2)}) async-start(), calls=%async_computation.10 | async-start | bytes 3899392 | tf_op jit(solution)/shard_map/reduce_scatter | solution.py:138
  238.9 0.8 copy-start.5
  239.7 9.8 %slice-start.2 = ((s8[6291456]{0:T(1024)(128)(4,1)}), s8[2097152]{0:T(1024)(128)(4,1)S(1)}, s32[]{:S(2)}) async-start(s8[6291456]{0:T(1024)(128)(4,1)} %bitcast.105), calls=%async_computation.13 | async-start | bytes 4194304
  240.5 5.1 %copy-start.3 = (bf16[16,384,64]{2,1,0:T(8,128)(2,1)S(1)}, bf16[16,384,64]{2,1,0:T(8,128)(2,1)}, u32[]{:S(2)}) copy-start(bf16[16,384,64]{2,1,0:T(8,128)(2,1)} %reshape_squeeze.25) | copy-start | bytes 2359300
  240.5 5.7 %copy-start.8 = (f32[16,32,2]{2,1,0:T(8,128)S(1)}, f32[16,32,2]{2,1,0:T(8,128)}, u32[]{:S(2)}) copy-start(f32[16,32,2]{2,1,0:T(8,128)} %copy.321) | copy-start | bytes 12292
  240.5 8.9 %slice-start.3 = ((s8[6291456]{0:T(1024)(128)(4,1)}), s8[4194304]{0:T(1024)(128)(4,1)S(1)}, s32[]{:S(2)}) async-start(s8[6291456]{0:T(1024)(128)(4,1)} %bitcast.105), calls=%async_computation.14 | async-start | bytes 8388608
  250.7 32.8 %copy-start.1 = (bf16[256,7168]{1,0:T(8,128)(2,1)S(1)}, bf16[256,7168]{1,0:T(8,128)(2,1)}, u32[]{:S(2)}) copy-start(bf16[256,7168]{1,0:T(8,128)(2,1)} %param.25) | copy-start | bytes 11010052
  286.4 0.7 copy-start.14
Sparse Core Ops, SparseCore 0:
  190.8 114.1 reduce-scatter.2
  307.6 96.7 reduce-scatter.4
where the time goes:
time: 414 us; the launch traced here: 413 us
  waiting for transfers between devices  169 us (41%)
  blocking collectives  152 us (37%)
  matrix products  22.2 us (5%)
  starting transfers between devices  21.8 us (5%)
  local copies, waits for them, and re-layouts  20.6 us (5%)
  between operations  14.7 us (4%)
  other arithmetic  13.1 us (3%)
    reduce_scatter x2, waiting for transfers between devices, local(): lax.psum_scatter(projected(jnp.int32(0), rows_here * lax.axis_size('tp'))...  115 us
    all_to_all x2, blocking collectives, local(): lax.all_to_all(attended, 'tp', split_axis=1, concat_axis=0, tiled=True)  50.6 us
    pmax x1, blocking collectives, local(): block_peak = lax.pmax(own_peak, 'tp')  45 us
    all_to_all x2, waiting for transfers between devices, local(): lax.all_to_all(query_lat, 'tp', split_axis=0, concat_axis=1, tiled=True)  41.3 us
    all_gather x1, blocking collectives, local(): lax.all_gather(bundle[1].astype(jnp.bfloat16), 'rep', axis=0, tiled=True)  31.1 us
    all_gather x1, blocking collectives, local(): lax.all_gather(bundle[0], 'rep', axis=0, tiled=True)  25 us
    all_to_all x2, waiting for transfers between devices, local(): lax.all_to_all(query_rope, 'tp', split_axis=0, concat_axis=1, tiled=True)  12.1 us
    all_to_all x2, starting transfers between devices, local(): lax.all_to_all(query_rope, 'tp', split_axis=0, concat_axis=1, tiled=True)  10.9 us
  transfers between devices with their start and end apart: 7, of which 6 were waited for; matrix products, arithmetic and copies ran while one was open for 7% of the time, Pallas kernels for 0%

commit v1 on v0

v1 whole, which is shorter than its diff:
```python
import jax
import jax.numpy as jnp
from jax import lax
from jax.experimental import pallas as pl
from jax.experimental.pallas import tpu as pltpu
from jax.sharding import PartitionSpec as P

HEADS = 32
LAT = 512
NOPE = 128
ROPE = 64
VDIM = 128
BLOCK = 128
STEPS = 2
D = 7168
LEN = 384
YS = 4
ZS = 4
TP = YS * ZS
REPS = 16
ROWS_DEV = 16
COLS = D // YS
EPSILON = 1e-06
SCALING = (NOPE + ROPE) ** (-0.5)
MESH = pl.DeviceIdType.MESH
BF = jnp.bfloat16
F32 = jnp.float32
VM = pl.BlockSpec(memory_space=pltpu.VMEM)
SM = pl.BlockSpec(memory_space=pltpu.SMEM)
ANY = pl.BlockSpec(memory_space=pl.ANY)


def rem(a, b):
    return lax.rem(a, jnp.int32(b))


def div(a, b):
    return lax.div(a, jnp.int32(b))


def rcopy(src, dst, send_sem, recv_sem, **where):
    return pltpu.make_async_remote_copy(
        src_ref=src,
        dst_ref=dst,
        send_sem=send_sem,
        recv_sem=recv_sem,
        device_id=where,
        device_id_type=MESH,
    )


def greet(tp_peers, rep_peers):
    barrier = pltpu.get_barrier_semaphore()
    for t in tp_peers:
        pl.semaphore_signal(barrier, inc=1, device_id={"tp": t}, device_id_type=MESH)
    for r in rep_peers:
        pl.semaphore_signal(barrier, inc=1, device_id={"rep": r}, device_id_type=MESH)
    pl.semaphore_wait(barrier, len(tp_peers) + len(rep_peers))


def mm(a, b, contract=((1,), (0,))):
    return lax.dot_general(a, b, (contract, ((), ())), preferred_element_type=F32)


def push_kernel(
    slot_ref,
    bver_ref,
    rver_ref,
    oscale_ref,
    tw_ref,
    ow_ref,
    sw_ref,
    ss_ref,
    dq_ref,
    gath,
    sel,
    buck,
    gsend,
    grecv,
    tsend,
    trecv,
    csend,
    crecv,
):
    rep, tp = lax.axis_index("rep"), lax.axis_index("tp")
    zh, x, c = div(rep, 8), rem(div(rep, 2), 4), rem(rep, 2)
    zpeer = rem(rep + 8, 16)
    cpeer = rep + 1 - 2 * c
    xpeers = [zh * 8 + rem(x + dx, 4) * 2 + c for dx in (1, 2, 3)]
    greet([rem(tp + k, TP) for k in range(1, TP)], [zpeer, cpeer] + xpeers)

    def block(b):
        return gath.at[pl.ds(2 * b, 2)]

    sent = []

    def send(src, b, to):
        copy = rcopy(src, block(b), gsend.at[len(sent)], grecv.at[b], rep=to)
        copy.start()
        sent.append(copy)

    def arrived(b):
        rcopy(block(b), block(b), gsend.at[0], grecv.at[b], rep=zpeer).wait_recv()

    for to in [zpeer] + xpeers + [cpeer]:
        send(tw_ref, rep, to)
    gath[pl.ds(2 * rep, 2)] = tw_ref[...]
    arrived(zpeer)
    for to in xpeers + [cpeer]:
        send(block(zpeer), zpeer, to)
    for xp in xpeers:
        arrived(xp)
        send(block(xp), xp, cpeer)
    for xp in xpeers:
        b = rem(xp + 8, 16)
        arrived(b)
        send(block(b), b, cpeer)
    for b in [cpeer, rem(cpeer + 8, 16)]:
        arrived(b)
    for xp in xpeers:
        other = xp + 1 - 2 * c
        arrived(other)
        arrived(rem(other + 8, 16))

    def part(src):
        return buck.at[c, pl.ds(pl.multiple_of(32 * src, 32), 32), :]

    def out_copy(k):
        t = rem(tp + k, TP)
        return rcopy(sel.at[k], part(tp), tsend.at[k], trecv.at[tp], tp=t)

    def pick(k, carry):
        t = rem(tp + k, TP)
        sel[k] = gath[slot_ref[2 * t + c]]
        out_copy(k).start()
        return carry

    lax.fori_loop(1, TP, pick, 0)
    buck[c, pl.ds(pl.multiple_of(32 * tp, 32), 32), :] = gath[slot_ref[2 * tp + c]]

    def take(k, carry):
        src = rem(tp + TP - k, TP)
        rcopy(part(src), part(src), tsend.at[k], trecv.at[src], tp=src).wait_recv()
        return carry

    lax.fori_loop(1, TP, take, 0)
    swap = rcopy(buck.at[c], buck.at[c], csend, crecv, rep=cpeer)
    swap.start()
    rcopy(buck.at[1 - c], buck.at[1 - c], csend, crecv, rep=cpeer).wait_recv()

    cell_row = lax.broadcasted_iota(jnp.int32, (4, 4), 0)
    cell_col = lax.broadcasted_iota(jnp.int32, (4, 4), 1)
    scales = jnp.zeros((4, 4), F32)
    for hh in range(2):
        head = 2 * tp + hh
        stale = (rver_ref[0, head] != bver_ref[head]).astype(jnp.int32)
        for i in range(4):
            for cc in range(2):
                rows = slice(i * BLOCK, (i + 1) * BLOCK)
                col = hh * 256 + cc * BLOCK
                raw = buck[hh, rows, cc * BLOCK : (cc + 1) * BLOCK].astype(F32)
                peak = jnp.max(jnp.abs(raw), axis=0, keepdims=True)
                peak = jnp.max(peak, axis=1, keepdims=True)
                scale = peak + EPSILON
                fresh = (raw / scale).astype(BF).astype(F32)
                old = ow_ref[0, rows, col : col + BLOCK].astype(F32)
                served = jnp.where(jnp.zeros((BLOCK, BLOCK), jnp.int32) + stale != 0, fresh, old)
                held = jnp.zeros((1, 1), F32) + oscale_ref[0, i, 2 * hh + cc]
                used = jnp.where(jnp.zeros((1, 1), jnp.int32) + stale != 0, scale, held)
                sw_ref[0, rows, col : col + BLOCK] = served.astype(BF)
                dq_ref[rows, col : col + BLOCK] = (served * used).astype(BF)
                here = (cell_row == i) & (cell_col == 2 * hh + cc)
                scales = jnp.where(here, used, scales)
    ss_ref[0] = scales

    for copy in sent:
        copy.wait_send()

    def drain(k, carry):
        out_copy(k).wait_send()
        return carry

    lax.fori_loop(1, TP, drain, 0)
    swap.wait_send()


def push(trainer_weight, bucket_slot, bucket_version, replica_version, old_weight, old_scale):
    dma = pltpu.SemaphoreType.DMA
    return pl.pallas_call(
        push_kernel,
        out_shape=(
            jax.ShapeDtypeStruct((1, LAT, 512), BF),
            jax.ShapeDtypeStruct((1, 4, 4), F32),
            jax.ShapeDtypeStruct((LAT, 512), BF),
        ),
        in_specs=[SM, SM, SM, SM, VM, VM],
        out_specs=(VM, VM, VM),
        scratch_shapes=[
            pltpu.VMEM((HEADS, 32, 256), BF),
            pltpu.VMEM((TP, 32, 256), BF),
            pltpu.VMEM((2, LAT, 256), BF),
            dma((15,)),
            dma((REPS,)),
            dma((TP,)),
            dma((TP,)),
            dma(()),
            dma(()),
        ],
        compiler_params=pltpu.CompilerParams(
            collective_id=0, has_side_effects=True, vmem_limit_bytes=24 * 2**20
        ),
        name="push",
    )(bucket_slot, bucket_version, replica_version, old_scale, trainer_weight, old_weight)


def attend_kernel(
    len_ref,
    dq_ref,
    qn_ref,
    qp_ref,
    rope_ref,
    tok_ref,
    cache_hbm,
    weight_hbm,
    ho_ref,
    wp,
    cache,
    perm,
    ropes,
    kr,
    toks,
    qs,
    qr,
    qrr,
    qrow,
    qro,
    attr,
    ab,
    ar,
    lsem,
    wsend,
    wrecv,
    xsend,
    xrecv,
    psend,
    precv,
    qsend,
    qrecv,
    asend,
    arecv,
):
    rep, tp = lax.axis_index("rep"), lax.axis_index("tp")
    y, z, c = div(tp, ZS), rem(tp, ZS), rem(rep, 2)
    cpeer = rep + 1 - 2 * c

    load = pltpu.make_async_copy(cache_hbm.at[0], cache, lsem.at[0])
    load.start()
    own_w = pltpu.make_async_copy(
        weight_hbm.at[:, pl.ds(pl.multiple_of(COLS * y, 256), COLS)], wp.at[y], lsem.at[1]
    )
    own_w.start()
    greet([rem(tp + k, TP) for k in range(1, TP)], [cpeer])

    def half(yy, side):
        return wp.at[yy, pl.ds(pl.multiple_of(128 * side, 128), 128), :]

    def rows16(t):
        return pl.ds(pl.multiple_of(16 * t, 16), 16)

    def rope_copy(k):
        t = rem(tp + k, TP)
        return rcopy(qp_ref.at[:, 0, rows16(t), :], qrr.at[:, tp], psend.at[k], precv.at[tp], tp=t)

    def query_copy(s, k):
        t = rem(tp + k, TP)
        return rcopy(
            qs.at[s, :, rows16(t), :], qr.at[s, :, tp], qsend.at[s, k], qrecv.at[s, tp], tp=t
        )

    def back_copy(s, k):
        t = rem(tp + k, TP)
        return rcopy(
            ab.at[s, :, t], ar.at[s, :, rows16(tp), :], asend.at[s, k], arecv.at[s, tp], tp=t
        )

    def weight_copy(dy):
        to = rem(y + dy, YS)
        src = weight_hbm.at[
            pl.ds(pl.multiple_of(128 * c, 128), 128), pl.ds(pl.multiple_of(COLS * to, 256), COLS)
        ]
        return rcopy(src, half(y, c), wsend.at[dy], wrecv.at[y], tp=to * ZS + z)

    def swap_copy(dy):
        src = rem(y + YS - dy, YS)
        return rcopy(half(src, c), half(src, c), xsend.at[dy], xrecv.at[src], rep=cpeer)

    def each(first, fn):
        def body(k, carry):
            fn(k)
            return carry

        lax.fori_loop(first, TP, body, 0)

    each(1, lambda k: rope_copy(k).start())
    for s in range(STEPS):
        for hh in range(2):
            qs[s, hh] = mm(
                qn_ref[s, 0, :, hh * NOPE : (hh + 1) * NOPE],
                dq_ref[:, hh * 256 : hh * 256 + NOPE],
                ((1,), (1,)),
            ).astype(BF)
        each(1, lambda k: query_copy(s, k).start())
    for dy in (1, 2, 3):
        weight_copy(dy).start()

    pi = lax.broadcasted_iota(jnp.int32, (256, 256), 0)
    pj = lax.broadcasted_iota(jnp.int32, (256, 256), 1)
    swapped = ((pi >> 4) == (pj & 15)) & ((pi & 15) == (pj >> 4))
    perm[...] = jnp.where(swapped, 1.0, 0.0).astype(BF)
    toks[...] = jnp.zeros_like(toks)
    toks[:, :, 0 : LAT + ROPE] = tok_ref[:, 0].astype(F32)
    for s in range(STEPS):
        qrr[s, tp] = qp_ref[s, 0, rows16(tp), :]
        for hh in range(2):
            qr[s, hh, tp] = qs[s, hh, rows16(tp), :]

    for g in range(12):
        tiles = [rope_ref[0, :, (16 * g + i) * 128 : (16 * g + i + 1) * 128] for i in range(16)]
        turned = mm(perm[...], jnp.concatenate(tiles, axis=0)).astype(BF)
        ropes[:, 16 * g : 16 * (g + 1), :] = turned.reshape(16, 16, 128)
    si = lax.broadcasted_iota(jnp.int32, (LEN, LEN // 2), 0)
    sj = lax.broadcasted_iota(jnp.int32, (LEN, LEN // 2), 1)
    spread = jnp.where((si >> 1) == sj, 1.0, 0.0).astype(BF)
    ki = lax.broadcasted_iota(jnp.int32, (LEN, 128), 0)
    kj = lax.broadcasted_iota(jnp.int32, (LEN, 128), 1)
    kept = (ki & 1) == (kj >> 6)

    def place(r, carry):
        kr[r] = jnp.where(kept, mm(spread, ropes[r]), 0.0).astype(BF)
        return carry

    lax.fori_loop(0, ROWS_DEV, place, 0)
    load.wait()

    di = lax.broadcasted_iota(jnp.int32, (128, 256), 0)
    dj = lax.broadcasted_iota(jnp.int32, (128, 256), 1)
    double = jnp.where(di == (dj >> 7) * 64 + (dj & 63), 1.0, 0.0).astype(BF)
    position = lax.broadcasted_iota(jnp.int32, (1, LEN), 1)

    def got_rope(k):
        src = rem(tp + TP - k, TP)
        rcopy(qrr.at[:, src], qrr.at[:, src], psend.at[k], precv.at[src], tp=src).wait_recv()

    each(1, got_rope)

    for s in range(STEPS):

        def got_query(k):
            src = rem(tp + TP - k, TP)
            there = qr.at[s, :, src]
            rcopy(there, there, qsend.at[s, k], qrecv.at[s, src], tp=src).wait_recv()

        each(1, got_query)
        for hh in range(2):
            turned = mm(perm[...], qr[s, hh].reshape(256, LAT)).astype(BF)
            qrow[:, 16 * hh : 16 * (hh + 1), :] = turned.reshape(16, 16, LAT)
        turned = mm(perm[...], qrr[s].reshape(256, 128)).astype(BF)
        turned = mm(turned, double).astype(BF)
        for hh in range(2):
            qro[:, 16 * hh : 16 * (hh + 1), :] = turned[:, 128 * hh : 128 * (hh + 1)].reshape(
                16, 16, 128
            )

        def attend_row(r, carry):
            q_lat, q_rope, keys = qrow[r], qro[r], cache[r]
            score = mm(q_lat, keys, ((1,), (1,))) + mm(q_rope, kr[r], ((1,), (1,)))
            score = jnp.where(position < len_ref[0, r], score * SCALING, -jnp.inf)
            top = jnp.max(score, axis=1, keepdims=True)
            lat32, rope32 = q_lat.astype(F32), q_rope.astype(F32)
            news = []
            for t in range(s + 1):
                tok = toks[t, pl.ds(r, 1), :]
                new = jnp.sum(lat32 * tok[:, :LAT], axis=1, keepdims=True)
                new = new + jnp.sum(rope32 * tok[:, LAT:], axis=1, keepdims=True)
                news.append((new * SCALING, tok[:, :LAT]))
            for new, _ in news:
                top = jnp.maximum(top, new)
            expped = jnp.exp(score - top)
            new_exp = [jnp.exp(new - top) for new, _ in news]
            total = jnp.sum(expped, axis=1, keepdims=True)
            for e in new_exp:
                total = total + e
            inverse = 1.0 / total
            out = mm((expped * inverse).astype(BF), keys)
            for e, (_, tok) in zip(new_exp, news):
                out = out + (e * inverse).astype(BF).astype(F32) * tok
            out = out.astype(BF)
            attr[0, r] = out[:16]
            attr[1, r] = out[16:]
            return carry

        lax.fori_loop(0, ROWS_DEV, attend_row, 0, unroll=4)
        for hh in range(2):
            turned = mm(perm[...], attr[hh].reshape(256, LAT)).astype(BF)
            ab[s, hh] = turned.reshape(16, 16, LAT)
        each(1, lambda k: back_copy(s, k).start())
        for hh in range(2):
            ar[s, hh, rows16(tp), :] = ab[s, hh, tp]

    for dy in (1, 2, 3):
        src = rem(y + YS - dy, YS)
        there = half(src, c)
        rcopy(there, there, wsend.at[dy], wrecv.at[src], tp=src * ZS + z).wait_recv()
        swap_copy(dy).start()

    for s in range(STEPS):

        def got_back(k):
            src = rem(tp + TP - k, TP)
            there = ar.at[s, :, rows16(src), :]
            rcopy(there, there, asend.at[s, k], arecv.at[s, src], tp=src).wait_recv()

        each(1, got_back)
        for hh in range(2):
            ho_ref[s, :, hh * VDIM : (hh + 1) * VDIM] = mm(
                ar[s, hh], dq_ref[:, hh * 256 + NOPE : (hh + 1) * 256]
            ).astype(BF)

    own_w.wait()
    for dy in (1, 2, 3):
        src = rem(y + YS - dy, YS)
        there = half(src, 1 - c)
        rcopy(there, there, xsend.at[dy], xrecv.at[src], rep=cpeer).wait_recv()
    for dy in (1, 2, 3):
        weight_copy(dy).wait_send()
        swap_copy(dy).wait_send()
    each(1, lambda k: rope_copy(k).wait_send())
    for s in range(STEPS):
        each(1, lambda k: query_copy(s, k).wait_send())
        each(1, lambda k: back_copy(s, k).wait_send())


def attend(dq, q_nope, q_rope, cache_latent, cache_rope, new_token, lengths, out_weight):
    dma = pltpu.SemaphoreType.DMA
    return pl.pallas_call(
        attend_kernel,
        out_shape=(
            jax.ShapeDtypeStruct((STEPS, 256, 256), BF),
            jax.ShapeDtypeStruct((YS, 256, COLS), BF),
        ),
        in_specs=[SM, VM, VM, VM, VM, VM, ANY, ANY],
        out_specs=(VM, VM),
        scratch_shapes=[
            pltpu.VMEM((ROWS_DEV, LEN, LAT), BF),
            pltpu.VMEM((256, 256), BF),
            pltpu.VMEM((ROWS_DEV, LEN // 2, 128), BF),
            pltpu.VMEM((ROWS_DEV, LEN, 128), BF),
            pltpu.VMEM((STEPS, ROWS_DEV, 640), F32),
            pltpu.VMEM((STEPS, 2, 256, LAT), BF),
            pltpu.VMEM((STEPS, 2, TP, 16, LAT), BF),
            pltpu.VMEM((STEPS, TP, 16, 128), BF),
            pltpu.VMEM((ROWS_DEV, HEADS, LAT), BF),
            pltpu.VMEM((ROWS_DEV, HEADS, 128), BF),
            pltpu.VMEM((2, ROWS_DEV, 16, LAT), BF),
            pltpu.VMEM((STEPS, 2, TP, 16, LAT), BF),
            pltpu.VMEM((STEPS, 2, 256, LAT), BF),
            dma((2,)),
            dma((YS,)),
            dma((YS,)),
            dma((YS,)),
            dma((YS,)),
            dma((TP,)),
            dma((TP,)),
            dma((STEPS, TP)),
            dma((STEPS, TP)),
            dma((STEPS, TP)),
            dma((STEPS, TP)),
        ],
        compiler_params=pltpu.CompilerParams(
            collective_id=1, has_side_effects=True, vmem_limit_bytes=48 * 2**20
        ),
        name="attend",
    )(lengths, dq, q_nope, q_rope, cache_rope, new_token, cache_latent, out_weight)


def project_kernel(
    ho_ref, wp, dec, hg, pb, r1, r2, sx, fin, hsend, hrecv, s1send, s1recv, s2send, s2recv, fsend, frecv
):
    tp = lax.axis_index("tp")
    y, z = div(tp, ZS), rem(tp, ZS)
    near = z + 1 - 2 * rem(z, 2)
    far = rem(z + 2, ZS)
    mirror = 3 - z
    peers = [rem(y + dy, YS) * ZS + z for dy in (1, 2, 3)]
    greet(peers + [y * ZS + near, y * ZS + far], [])

    def gather_copy(s, dy):
        to = rem(y + dy, YS) * ZS + z
        return rcopy(ho_ref.at[s], hg.at[s, y], hsend.at[s, dy], hrecv.at[s, y], tp=to)

    def near_copy(s, which):
        blk = mirror if which == 0 else near
        return rcopy(
            pb.at[s, :, blk], r1.at[s, which], s1send.at[s, which], s1recv.at[s, which], tp=y * ZS + near
        )

    def far_copy(s):
        return rcopy(sx.at[s], r2.at[s], s2send.at[s], s2recv.at[s], tp=y * ZS + far)

    def home_copy(s, dy):
        to = rem(y + dy, YS)
        there = dec.at[s, 0, :, pl.ds(pl.multiple_of(COLS * y, 256), COLS)]
        return rcopy(fin.at[s, to], there, fsend.at[s, dy], frecv.at[s, y], tp=to * ZS + z)

    for s in range(STEPS):
        for dy in (1, 2, 3):
            gather_copy(s, dy).start()
        hg[s, y] = ho_ref[s]

    for s in range(STEPS):
        for dy in (1, 2, 3):
            src = rem(y + YS - dy, YS)
            there = hg.at[s, src]
            rcopy(there, there, hsend.at[s, dy], hrecv.at[s, src], tp=src * ZS + z).wait_recv()

        def columns(n, carry):
            cols = pl.ds(pl.multiple_of(256 * n, 256), 256)
            total = mm(hg[s, 0], wp[0, :, cols])
            for k in range(1, YS):
                total = total + mm(hg[s, k], wp[k, :, cols])
            pb[s, :, :, :, cols] = total.astype(BF).reshape(YS, ZS, 16, 256)
            return carry

        lax.fori_loop(0, COLS // 256, columns, 0)
        for which in range(2):
            near_copy(s, which).start()

    for s in range(STEPS):
        near_copy(s, 0).wait_recv()
        sx[s] = (pb[s, :, far].astype(F32) + r1[s, 0].astype(F32)).astype(BF)
        far_copy(s).start()

    for s in range(STEPS):
        near_copy(s, 1).wait_recv()
        far_copy(s).wait_recv()
        fin[s] = (
            pb[s, :, z].astype(F32) + r1[s, 1].astype(F32) + r2[s].astype(F32)
        ).astype(BF)
        for dy in (1, 2, 3):
            home_copy(s, dy).start()
        dec[s, 0, :, pl.ds(pl.multiple_of(COLS * y, 256), COLS)] = fin[s, y]

    for s in range(STEPS):
        for dy in (1, 2, 3):
            src = rem(y + YS - dy, YS)
            there = dec.at[s, 0, :, pl.ds(pl.multiple_of(COLS * src, 256), COLS)]
            rcopy(there, there, fsend.at[s, dy], frecv.at[s, src], tp=src * ZS + z).wait_recv()
    for s in range(STEPS):
        for dy in (1, 2, 3):
            gather_copy(s, dy).wait_send()
            home_copy(s, dy).wait_send()
        for which in range(2):
            near_copy(s, which).wait_send()
        far_copy(s).wait_send()


def project(ho, wp):
    dma = pltpu.SemaphoreType.DMA
    block = (STEPS, YS, 16, COLS)
    return pl.pallas_call(
        project_kernel,
        out_shape=jax.ShapeDtypeStruct((STEPS, 1, 16, D), BF),
        in_specs=[VM, VM],
        out_specs=VM,
        scratch_shapes=[
            pltpu.VMEM((STEPS, YS, 256, 256), BF),
            pltpu.VMEM((STEPS, YS, ZS, 16, COLS), BF),
            pltpu.VMEM((STEPS, 2, YS, 16, COLS), BF),
            pltpu.VMEM(block, BF),
            pltpu.VMEM(block, BF),
            pltpu.VMEM(block, BF),
            dma((STEPS, YS)),
            dma((STEPS, YS)),
            dma((STEPS, 2)),
            dma((STEPS, 2)),
            dma((STEPS,)),
            dma((STEPS,)),
            dma((STEPS, YS)),
            dma((STEPS, YS)),
        ],
        compiler_params=pltpu.CompilerParams(
            collective_id=2, has_side_effects=True, vmem_limit_bytes=40 * 2**20
        ),
        name="project",
    )(ho, wp)


def local(
    trainer_weight,
    bucket_slot,
    bucket_version,
    replica_version,
    old_weight,
    old_scale,
    q_nope,
    q_rope,
    cache_latent,
    cache_rope,
    new_token,
    lengths,
    out_weight,
):
    served_weight, served_scale, dq = push(
        trainer_weight, bucket_slot, bucket_version, replica_version, old_weight, old_scale
    )
    ho, wp = attend(
        dq, q_nope, q_rope, cache_latent, cache_rope, new_token, lengths, out_weight
    )
    decoded = project(ho, wp)
    return (served_weight, served_scale, decoded)


def solution(mesh):
    return jax.shard_map(
        local,
        mesh=mesh,
        in_specs=(
            P("rep", "tp", None),
            P(),
            P(),
            P("rep", None),
            P("rep", None, "tp"),
            P("rep", None, "tp"),
            P(None, "rep", None, "tp"),
            P(None, "rep", None, "tp"),
            P("rep", "tp", None, None),
            P("rep", "tp", None),
            P(None, "rep", "tp", None),
            P("rep", "tp"),
            P("tp", None),
        ),
        out_specs=(P("rep", None, "tp"), P("rep", None, "tp"), P(None, "rep", "tp", None)),
        check_vma=False,
    )
```

time: 414 us -> 152 us (0.37)
  waiting for transfers between devices: 169 us -> 0 us
  blocking collectives: 152 us -> 0 us
  Pallas kernels: 0 us -> 138 us
  matrix products: 22.2 us -> 0 us
  starting transfers between devices: 21.8 us -> 0 us
  between operations: 14.7 us -> 0.68 us
  other arithmetic: 13.1 us -> 0 us
  local copies, waits for them, and re-layouts: 20.6 us -> 11 us
    pallas_call x0 -> x3, Pallas kernels: none -> 138 us  [the longest x1 56.8 us: attend(): pl.pallas_call(attend_kernel, out_shape=(jax.ShapeDtypeStruct((STEPS, 256...]
    reduce_scatter x2 -> x0, waiting for transfers between devices: 115 us -> none  [local(): lax.psum_scatter(projected(jnp.int32(0), rows_here * lax.axis_size('tp'))...]
    all_gather x2 -> x0, blocking collectives: 56.1 us -> none  [the longest x1 31.1 us: local(): lax.all_gather(bundle[1].astype(jnp.bfloat16), 'rep', axis=0, tiled=True)]
    all_to_all x5 -> x0, waiting for transfers between devices: 53.4 us -> none  [the longest x2 41.3 us: local(): lax.all_to_all(query_lat, 'tp', split_axis=0, concat_axis=1, tiled=True)]
    all_to_all x2 -> x0, blocking collectives: 50.6 us -> none  [local(): lax.all_to_all(attended, 'tp', split_axis=1, concat_axis=0, tiled=True)]
    pmax x1 -> x0, blocking collectives: 45 us -> none  [local(): block_peak = lax.pmax(own_peak, 'tp')]
    dot_general x18 -> x0, matrix products: 22.2 us -> none  [the longest x2 10.1 us: attend(): jnp.einsum('rhl,rjl->rhj', row_lat, keys_lat, preferred_element_type=jnp....]
    all_to_all x5 -> x0, starting transfers between devices: 21.6 us -> none  [the longest x2 10.9 us: local(): lax.all_to_all(query_rope, 'tp', split_axis=0, concat_axis=1, tiled=True)]
  transfers between devices with their start and end apart: 7 -> 0, of which waited for: 6 -> 0; matrix products, arithmetic and copies ran while one was open for 7% -> 0% of each run, Pallas kernels for 0% -> 0%
where the time goes in v1:
time: 152 us; the launch traced here: 150 us
  Pallas kernels  138 us (91%)
  local copies, waits for them, and re-layouts  11 us (7%)
    pallas_call x1, Pallas kernels, attend(): pl.pallas_call(attend_kernel, out_shape=(jax.ShapeDtypeStruct((STEPS, 256...  56.8 us
    pallas_call x1, Pallas kernels, project(): pl.pallas_call(project_kernel, out_shape=jax.ShapeDtypeStruct((STEPS, 1,...  53.6 us
    pallas_call x1, Pallas kernels, push(): pl.pallas_call(push_kernel, out_shape=(jax.ShapeDtypeStruct((1, LAT, 512)...  27.9 us
    unnamed x25, local copies, waits for them, and re-layouts  11 us

profile of v1, /device:TPU:4, one launch (start us, length us, event | category | flops | bytes accessed | tf_op | source)
XLA Modules:
  0.0 150.0 jit_solution(6229068107005248332)
XLA Ops:
  0.6 0.0 copy-start.1
  0.6 1.0 copy-done.1
  1.7 0.0 copy-start.5
  1.7 0.8 copy-done.5
  2.4 0.0 copy-start.6
  2.4 0.7 copy-done.6
  3.1 0.0 copy-start.7
  3.1 0.7 copy-done.7
  3.8 0.0 copy-start.8
  3.8 0.7 copy-done.8
  4.4 0.0 copy-start.9
  4.4 0.7 copy-done.9
  5.1 27.9 %push.1 = (bf16[1,512,512]{2,1,0:T(8,128)(2,1)S(1)}, f32[1,4,4]{2,1,0:T(4,128)S(1)}, bf16[512,512]{1,0:T(8,128)(2,1)S(1)}) custom-call(s32[32]{0:T(128)S(1)} %copy-done.7, s32[32]{0:T(128)S(1)} %copy-done.8, s32[1,32]{1,0:T(1,128)S(1)} %copy-done.9, f32[1,4,4]{2,1,0:T(4,128)S(1)} %copy-done.6, bf16[2,32,256]{2,1,0:T(8,128)(2,1)S(1)} %copy-done.5, ...), custom_call_target="tpu_custom_call" | custom-call | tf_op jit(solution)/shard_map/push/pallas_call | solution.py:189
  33.0 0.0 copy-start
  33.0 1.1 copy-done
  34.1 0.0 copy-start.2
  34.1 0.9 copy-done.2
  35.1 0.0 copy-start.3
  35.1 0.9 copy-done.3
  36.0 0.0 copy-start.4
  36.0 0.8 copy-done.4
  36.7 0.0 copy-start.10
  36.7 0.7 copy-done.10
  37.4 56.8 %attend.1 = (bf16[2,256,256]{2,1,0:T(8,128)(2,1)S(1)}, bf16[4,256,1792]{2,1,0:T(8,128)(2,1)S(1)}) custom-call(s32[1,16]{1,0:T(1,128)S(1)} %copy-done.10, bf16[512,512]{1,0:T(8,128)(2,1)S(1)} %get-tuple-element.10.dq_ref, bf16[2,1,256,256]{3,2,1,0:T(8,128)(2,1)S(1)} %copy-done.2, bf16[2,1,256,128]{3,2,1,0:T(8,128)(2,1)S(1)} %copy-done.3, ...), custom_call_target="tpu_custom_call" | custom-call | tf_op jit(solution)/shard_map/attend/pallas_call | solution.py:445
  94.2 53.6 %project.1 = bf16[2,1,16,7168]{3,2,1,0:T(8,128)(2,1)S(1)} custom-call(bf16[2,256,256]{2,1,0:T(8,128)(2,1)S(1)} %get-tuple-element.11.ho_ref, bf16[4,256,1792]{2,1,0:T(8,128)(2,1)S(1)} %get-tuple-element.12.wp), custom_call_target="tpu_custom_call" | custom-call | tf_op jit(solution)/shard_map/project/pallas_call | solution.py:570
  147.8 0.8 copy.19
  148.6 0.6 copy.20
  149.2 0.8 copy.21
Async XLA Ops:
  0.6 1.0 copy-start.1
  1.7 0.8 copy-start.5
  2.4 0.7 copy-start.6
  3.1 0.7 copy-start.7
  3.8 0.7 copy-start.8
  4.4 0.7 copy-start.9
  33.0 1.1 copy-start
  34.1 0.9 copy-start.2
  35.1 0.9 copy-start.3
  36.0 0.8 copy-start.4
  36.7 0.7 copy-start.10

commit v2 on v0

v2 whole, which is shorter than its diff:
```python
import jax
import jax.numpy as jnp
from jax import lax
from jax.experimental import pallas as pl
from jax.experimental.pallas import tpu as pltpu
from jax.sharding import PartitionSpec as P

HEADS = 32
LAT = 512
NOPE = 128
ROPE = 64
VDIM = 128
BLOCK = 128
STEPS = 2
D = 7168
LEN = 384
YS = 4
ZS = 4
TP = YS * ZS
REPS = 16
ROWS_DEV = 16
COLS = D // YS
HALF = COLS // 2
CHUNKS = 4
EPSILON = 1e-06
SCALING = (NOPE + ROPE) ** (-0.5)
MESH = pl.DeviceIdType.MESH
BF = jnp.bfloat16
F32 = jnp.float32
VM = pl.BlockSpec(memory_space=pltpu.VMEM)
SM = pl.BlockSpec(memory_space=pltpu.SMEM)
ANY = pl.BlockSpec(memory_space=pl.ANY)


def rem(a, b):
    return lax.rem(a, jnp.int32(b))


def div(a, b):
    return lax.div(a, jnp.int32(b))


def rcopy(src, dst, send_sem, recv_sem, **where):
    return pltpu.make_async_remote_copy(
        src_ref=src,
        dst_ref=dst,
        send_sem=send_sem,
        recv_sem=recv_sem,
        device_id=where,
        device_id_type=MESH,
    )


def greet(tp_peers, rep_peers):
    barrier = pltpu.get_barrier_semaphore()
    for t in tp_peers:
        pl.semaphore_signal(barrier, inc=1, device_id={"tp": t}, device_id_type=MESH)
    for r in rep_peers:
        pl.semaphore_signal(barrier, inc=1, device_id={"rep": r}, device_id_type=MESH)
    pl.semaphore_wait(barrier, len(tp_peers) + len(rep_peers))


def mm(a, b, contract=((1,), (0,))):
    return lax.dot_general(a, b, (contract, ((), ())), preferred_element_type=F32)


def everything(
    slot_ref,
    bver_ref,
    rver_ref,
    oscale_ref,
    len_ref,
    tw_hbm,
    ow_hbm,
    qn_hbm,
    qp_hbm,
    cache_hbm,
    rope_hbm,
    tok_hbm,
    weight_hbm,
    sw_ref,
    ss_ref,
    dec,
    gath,
    sel,
    buck,
    ow,
    dq,
    qn,
    rope,
    tok,
    cache,
    wp,
    perm,
    ropes,
    kr,
    toks,
    qs,
    qr,
    qrr,
    qrow,
    qro,
    attr,
    ab,
    ar,
    ho,
    hg,
    pb,
    r1,
    r2,
    sx,
    fin,
    lsem,
    gsend,
    grecv,
    tsend,
    trecv,
    csend,
    crecv,
    wsend,
    wrecv,
    xsend,
    xrecv,
    psend,
    precv,
    qsend,
    qrecv,
    asend,
    arecv,
    hsend,
    hrecv,
    s1send,
    s1recv,
    s2send,
    s2recv,
    fsend,
    frecv,
):
    rep, tp = lax.axis_index("rep"), lax.axis_index("tp")
    zh, x, c = div(rep, 8), rem(div(rep, 2), 4), rem(rep, 2)
    y, z = div(tp, ZS), rem(tp, ZS)
    zpeer = rem(rep + 8, 16)
    cpeer = rep + 1 - 2 * c
    xpeers = [zh * 8 + rem(x + dx, 4) * 2 + c for dx in (1, 2, 3)]
    near = z + 1 - 2 * rem(z, 2)
    far = rem(z + 2, ZS)
    mirror = 3 - z

    def rows16(t):
        return pl.ds(pl.multiple_of(16 * t, 16), 16)

    def rows32(t):
        return pl.ds(pl.multiple_of(32 * t, 32), 32)

    def columns(yy):
        return pl.ds(pl.multiple_of(COLS * yy, 256), COLS)

    def each(fn):
        def body(k, carry):
            fn(k)
            return carry

        lax.fori_loop(1, TP, body, 0)

    def source(k):
        return rem(tp + TP - k, TP)

    loads = [
        pltpu.make_async_copy(src, dst, lsem.at[i])
        for i, (src, dst) in enumerate(
            [
                (tw_hbm, gath.at[pl.ds(2 * rep, 2)]),
                (qp_hbm.at[:, 0, rows16(tp), :], qrr.at[:, tp]),
                (tok_hbm.at[:, 0], tok),
                (rope_hbm.at[0], rope),
                (ow_hbm.at[0], ow),
                (qn_hbm.at[:, 0], qn),
                (cache_hbm.at[0], cache),
                (weight_hbm.at[:, columns(y)], wp.at[y]),
            ]
        )
    ]
    load_tw, load_qp, load_tok, load_rope, load_ow, load_qn, load_cache, load_w = loads
    for copy in loads:
        copy.start()
    greet([rem(tp + k, TP) for k in range(1, TP)], [zpeer, cpeer] + xpeers)

    def block(b):
        return gath.at[pl.ds(2 * b, 2)]

    sent = []

    def pass_on(src, b, to):
        copy = rcopy(src, block(b), gsend.at[len(sent)], grecv.at[b], rep=to)
        copy.start()
        sent.append(copy)

    def arrived(b):
        rcopy(block(b), block(b), gsend.at[0], grecv.at[b], rep=zpeer).wait_recv()

    def part(src):
        return buck.at[c, rows32(src), :]

    def pick_copy(k):
        t = rem(tp + k, TP)
        return rcopy(sel.at[k], part(tp), tsend.at[k], trecv.at[tp], tp=t)

    def half(yy, side):
        return wp.at[yy, pl.ds(pl.multiple_of(128 * side, 128), 128), :]

    def weight_copy(dy):
        to = rem(y + dy, YS)
        src = weight_hbm.at[pl.ds(pl.multiple_of(128 * c, 128), 128), columns(to)]
        return rcopy(src, half(y, c), wsend.at[dy], wrecv.at[y], tp=to * ZS + z)

    def swap_copy(dy):
        src = rem(y + YS - dy, YS)
        return rcopy(half(src, c), half(src, c), xsend.at[dy], xrecv.at[src], rep=cpeer)

    def rope_copy(k):
        t = rem(tp + k, TP)
        return rcopy(qp_hbm.at[:, 0, rows16(t), :], qrr.at[:, tp], psend.at[k], precv.at[tp], tp=t)

    def query_copy(s, k):
        t = rem(tp + k, TP)
        return rcopy(
            qs.at[s, :, rows16(t), :], qr.at[s, :, tp], qsend.at[s, k], qrecv.at[s, tp], tp=t
        )

    def back_copy(s, k):
        t = rem(tp + k, TP)
        return rcopy(
            ab.at[s, :, t], ar.at[s, :, rows16(tp), :], asend.at[s, k], arecv.at[s, tp], tp=t
        )

    def gather_copy(s, dy):
        to = rem(y + dy, YS) * ZS + z
        return rcopy(ho.at[s], hg.at[s, y], hsend.at[s, dy], hrecv.at[s, y], tp=to)

    def near_copy(q, which):
        blk = mirror if which == 0 else near
        return rcopy(
            pb.at[q, :, blk], r1.at[q, which], s1send.at[q, which], s1recv.at[q, which], tp=y * ZS + near
        )

    def far_copy(q):
        return rcopy(sx.at[q], r2.at[q], s2send.at[q], s2recv.at[q], tp=y * ZS + far)

    def home(q, yy):
        first = pl.multiple_of(COLS * yy + HALF * (q % 2), 128)
        return dec.at[q // 2, 0, :, pl.ds(first, HALF)]

    def home_copy(q, dy):
        to = rem(y + dy, YS)
        return rcopy(fin.at[q, to], home(q, y), fsend.at[q, dy], frecv.at[q, y], tp=to * ZS + z)

    for to in [zpeer] + xpeers + [cpeer]:
        pass_on(tw_hbm, rep, to)
    weight_copy(1).start()
    weight_copy(3).start()
    arrived(zpeer)
    for to in xpeers + [cpeer]:
        pass_on(block(zpeer), zpeer, to)
    for xp in xpeers:
        arrived(xp)
        pass_on(block(xp), xp, cpeer)
    for xp in xpeers:
        b = rem(xp + 8, 16)
        arrived(b)
        pass_on(block(b), b, cpeer)
    load_tw.wait()
    for b in [cpeer, rem(cpeer + 8, 16)]:
        arrived(b)
    for xp in xpeers:
        other = xp + 1 - 2 * c
        arrived(other)
        arrived(rem(other + 8, 16))

    def pick(k):
        sel[k] = gath[slot_ref[2 * rem(tp + k, TP) + c]]
        pick_copy(k).start()

    each(pick)
    buck[c, rows32(tp), :] = gath[slot_ref[2 * tp + c]]
    each(lambda k: rope_copy(k).start())
    weight_copy(2).start()

    pi = lax.broadcasted_iota(jnp.int32, (256, 256), 0)
    pj = lax.broadcasted_iota(jnp.int32, (256, 256), 1)
    swapped = ((pi >> 4) == (pj & 15)) & ((pi & 15) == (pj >> 4))
    perm[...] = jnp.where(swapped, 1.0, 0.0).astype(BF)
    load_tok.wait()
    toks[...] = jnp.zeros_like(toks)
    toks[:, :, 0 : LAT + ROPE] = tok[...].astype(F32)
    load_rope.wait()
    for g in range(12):
        tiles = [rope[:, (16 * g + i) * 128 : (16 * g + i + 1) * 128] for i in range(16)]
        turned = mm(perm[...], jnp.concatenate(tiles, axis=0)).astype(BF)
        ropes[:, 16 * g : 16 * (g + 1), :] = turned.reshape(16, 16, 128)

    def bucket_arrived(k):
        src = source(k)
        rcopy(part(src), part(src), tsend.at[k], trecv.at[src], tp=src).wait_recv()

    each(bucket_arrived)
    swap = rcopy(buck.at[c], buck.at[c], csend, crecv, rep=cpeer)
    swap.start()
    load_ow.wait()
    load_qn.wait()
    rcopy(buck.at[1 - c], buck.at[1 - c], csend, crecv, rep=cpeer).wait_recv()

    cell_row = lax.broadcasted_iota(jnp.int32, (4, 4), 0)
    cell_col = lax.broadcasted_iota(jnp.int32, (4, 4), 1)

    def serve(hh, cc, scales):
        head = 2 * tp + hh
        stale = (rver_ref[0, head] != bver_ref[head]).astype(jnp.int32)
        col = hh * 256 + cc * BLOCK
        for i in range(4):
            rows = slice(i * BLOCK, (i + 1) * BLOCK)
            raw = buck[hh, rows, cc * BLOCK : (cc + 1) * BLOCK].astype(F32)
            peak = jnp.max(jnp.abs(raw), axis=0, keepdims=True)
            peak = jnp.max(peak, axis=1, keepdims=True)
            scale = peak + EPSILON
            fresh = (raw / scale).astype(BF).astype(F32)
            old = ow[rows, col : col + BLOCK].astype(F32)
            served = jnp.where(jnp.zeros((BLOCK, BLOCK), jnp.int32) + stale != 0, fresh, old)
            held = jnp.zeros((1, 1), F32) + oscale_ref[0, i, 2 * hh + cc]
            used = jnp.where(jnp.zeros((1, 1), jnp.int32) + stale != 0, scale, held)
            sw_ref[0, rows, col : col + BLOCK] = served.astype(BF)
            dq[rows, col : col + BLOCK] = (served * used).astype(BF)
            here = (cell_row == i) & (cell_col == 2 * hh + cc)
            scales = jnp.where(here, used, scales)
        return scales

    scales = jnp.zeros((4, 4), F32)
    for hh in range(2):
        scales = serve(hh, 0, scales)

    for s in range(STEPS):
        for hh in range(2):
            qs[s, hh] = mm(
                qn[s, :, hh * NOPE : (hh + 1) * NOPE],
                dq[:, hh * 256 : hh * 256 + NOPE],
                ((1,), (1,)),
            ).astype(BF)
        each(lambda k: query_copy(s, k).start())
    for hh in range(2):
        scales = serve(hh, 1, scales)
    ss_ref[0] = scales
    for s in range(STEPS):
        for hh in range(2):
            qr[s, hh, tp] = qs[s, hh, rows16(tp), :]

    si = lax.broadcasted_iota(jnp.int32, (LEN, LEN // 2), 0)
    sj = lax.broadcasted_iota(jnp.int32, (LEN, LEN // 2), 1)
    spread = jnp.where((si >> 1) == sj, 1.0, 0.0).astype(BF)
    ki = lax.broadcasted_iota(jnp.int32, (LEN, 128), 0)
    kj = lax.broadcasted_iota(jnp.int32, (LEN, 128), 1)
    kept = (ki & 1) == (kj >> 6)

    def place(r, carry):
        kr[r] = jnp.where(kept, mm(spread, ropes[r]), 0.0).astype(BF)
        return carry

    lax.fori_loop(0, ROWS_DEV, place, 0)
    load_cache.wait()
    load_qp.wait()

    di = lax.broadcasted_iota(jnp.int32, (128, 256), 0)
    dj = lax.broadcasted_iota(jnp.int32, (128, 256), 1)
    double = jnp.where(di == (dj >> 7) * 64 + (dj & 63), 1.0, 0.0).astype(BF)
    position = lax.broadcasted_iota(jnp.int32, (1, LEN), 1)

    def rope_arrived(k):
        src = source(k)
        rcopy(qrr.at[:, src], qrr.at[:, src], psend.at[k], precv.at[src], tp=src).wait_recv()

    each(rope_arrived)

    for s in range(STEPS):

        def query_arrived(k):
            src = source(k)
            there = qr.at[s, :, src]
            rcopy(there, there, qsend.at[s, k], qrecv.at[s, src], tp=src).wait_recv()

        turned = mm(perm[...], qrr[s].reshape(256, 128)).astype(BF)
        turned = mm(turned, double).astype(BF)
        for hh in range(2):
            qro[:, 16 * hh : 16 * (hh + 1), :] = turned[:, 128 * hh : 128 * (hh + 1)].reshape(
                16, 16, 128
            )
        each(query_arrived)
        for hh in range(2):
            turned = mm(perm[...], qr[s, hh].reshape(256, LAT)).astype(BF)
            qrow[:, 16 * hh : 16 * (hh + 1), :] = turned.reshape(16, 16, LAT)

        def attend_row(r, carry):
            q_lat, q_rope, keys = qrow[r], qro[r], cache[r]
            score = mm(q_lat, keys, ((1,), (1,))) + mm(q_rope, kr[r], ((1,), (1,)))
            score = jnp.where(position < len_ref[0, r], score * SCALING, -jnp.inf)
            top = jnp.max(score, axis=1, keepdims=True)
            lat32, rope32 = q_lat.astype(F32), q_rope.astype(F32)
            news = []
            for t in range(s + 1):
                tok_r = toks[t, pl.ds(r, 1), :]
                new = jnp.sum(lat32 * tok_r[:, :LAT], axis=1, keepdims=True)
                new = new + jnp.sum(rope32 * tok_r[:, LAT:], axis=1, keepdims=True)
                news.append((new * SCALING, tok_r[:, :LAT]))
            for new, _ in news:
                top = jnp.maximum(top, new)
            expped = jnp.exp(score - top)
            new_exp = [jnp.exp(new - top) for new, _ in news]
            total = jnp.sum(expped, axis=1, keepdims=True)
            for e in new_exp:
                total = total + e
            inverse = 1.0 / total
            out = mm((expped * inverse).astype(BF), keys)
            for e, (_, tok_r) in zip(new_exp, news):
                out = out + (e * inverse).astype(BF).astype(F32) * tok_r
            out = out.astype(BF)
            attr[0, r] = out[:16]
            attr[1, r] = out[16:]
            return carry

        lax.fori_loop(0, ROWS_DEV, attend_row, 0, unroll=4)
        for hh in range(2):
            turned = mm(perm[...], attr[hh].reshape(256, LAT)).astype(BF)
            ab[s, hh] = turned.reshape(16, 16, LAT)
        each(lambda k: back_copy(s, k).start())
        for hh in range(2):
            ar[s, hh, rows16(tp), :] = ab[s, hh, tp]
        if s == 0:
            for dy in (1, 2, 3):
                src = rem(y + YS - dy, YS)
                there = half(src, c)
                rcopy(there, there, wsend.at[dy], wrecv.at[src], tp=src * ZS + z).wait_recv()
                swap_copy(dy).start()

    load_w.wait()
    for dy in (1, 2, 3):
        src = rem(y + YS - dy, YS)
        there = half(src, 1 - c)
        rcopy(there, there, xsend.at[dy], xrecv.at[src], rep=cpeer).wait_recv()

    def heads_out(s):
        def back_arrived(k):
            src = source(k)
            there = ar.at[s, :, rows16(src), :]
            rcopy(there, there, asend.at[s, k], arecv.at[s, src], tp=src).wait_recv()

        each(back_arrived)
        for hh in range(2):
            ho[s, :, hh * VDIM : (hh + 1) * VDIM] = mm(
                ar[s, hh], dq[:, hh * 256 + NOPE : (hh + 1) * 256]
            ).astype(BF)
        for dy in (1, 2, 3):
            gather_copy(s, dy).start()
        hg[s, y] = ho[s]

    def multiply(s):
        for dy in (1, 2, 3):
            src = rem(y + YS - dy, YS)
            there = hg.at[s, src]
            rcopy(there, there, hsend.at[s, dy], hrecv.at[s, src], tp=src * ZS + z).wait_recv()
        for q in (2 * s, 2 * s + 1):
            for first, width in ((0, 512), (512, 384)):
                cols = slice(HALF * (q % 2) + first, HALF * (q % 2) + first + width)
                total = mm(hg[s, 0], wp[0, :, cols])
                for k in range(1, YS):
                    total = total + mm(hg[s, k], wp[k, :, cols])
                pb[q, :, :, :, first : first + width] = total.astype(BF).reshape(YS, ZS, 16, width)
            for which in range(2):
                near_copy(q, which).start()

    def cross(q):
        near_copy(q, 0).wait_recv()
        sx[q] = (pb[q, :, far].astype(F32) + r1[q, 0].astype(F32)).astype(BF)
        far_copy(q).start()

    def finish(q):
        near_copy(q, 1).wait_recv()
        far_copy(q).wait_recv()
        fin[q] = (pb[q, :, z].astype(F32) + r1[q, 1].astype(F32) + r2[q].astype(F32)).astype(BF)
        for dy in (1, 2, 3):
            home_copy(q, dy).start()
        first = pl.multiple_of(COLS * y + HALF * (q % 2), 128)
        dec[q // 2, 0, :, pl.ds(first, HALF)] = fin[q, y]

    heads_out(0)
    multiply(0)
    heads_out(1)
    cross(0)
    multiply(1)
    cross(1)
    finish(0)
    cross(2)
    finish(1)
    cross(3)
    finish(2)
    finish(3)

    for q in range(CHUNKS):
        for dy in (1, 2, 3):
            src = rem(y + YS - dy, YS)
            rcopy(
                home(q, src), home(q, src), fsend.at[q, dy], frecv.at[q, src], tp=src * ZS + z
            ).wait_recv()

    for copy in sent:
        copy.wait_send()
    each(lambda k: pick_copy(k).wait_send())
    swap.wait_send()
    each(lambda k: rope_copy(k).wait_send())
    for dy in (1, 2, 3):
        weight_copy(dy).wait_send()
        swap_copy(dy).wait_send()
    for s in range(STEPS):
        each(lambda k: query_copy(s, k).wait_send())
        each(lambda k: back_copy(s, k).wait_send())
        for dy in (1, 2, 3):
            gather_copy(s, dy).wait_send()
    for q in range(CHUNKS):
        for which in range(2):
            near_copy(q, which).wait_send()
        far_copy(q).wait_send()
        for dy in (1, 2, 3):
            home_copy(q, dy).wait_send()


def local(
    trainer_weight,
    bucket_slot,
    bucket_version,
    replica_version,
    old_weight,
    old_scale,
    q_nope,
    q_rope,
    cache_latent,
    cache_rope,
    new_token,
    lengths,
    out_weight,
):
    dma = pltpu.SemaphoreType.DMA
    chunk = (CHUNKS, YS, 16, HALF)
    return pl.pallas_call(
        everything,
        out_shape=(
            jax.ShapeDtypeStruct((1, LAT, 512), BF),
            jax.ShapeDtypeStruct((1, 4, 4), F32),
            jax.ShapeDtypeStruct((STEPS, 1, 16, D), BF),
        ),
        in_specs=[SM] * 5 + [ANY] * 8,
        out_specs=(VM, VM, VM),
        scratch_shapes=[
            pltpu.VMEM((HEADS, 32, 256), BF),
            pltpu.VMEM((TP, 32, 256), BF),
            pltpu.VMEM((2, LAT, 256), BF),
            pltpu.VMEM((LAT, 512), BF),
            pltpu.VMEM((LAT, 512), BF),
            pltpu.VMEM((STEPS, 256, 256), BF),
            pltpu.VMEM((ROWS_DEV, LEN * ROPE), BF),
            pltpu.VMEM((STEPS, ROWS_DEV, LAT + ROPE), BF),
            pltpu.VMEM((ROWS_DEV, LEN, LAT), BF),
            pltpu.VMEM((YS, 256, COLS), BF),
            pltpu.VMEM((256, 256), BF),
            pltpu.VMEM((ROWS_DEV, LEN // 2, 128), BF),
            pltpu.VMEM((ROWS_DEV, LEN, 128), BF),
            pltpu.VMEM((STEPS, ROWS_DEV, 640), F32),
            pltpu.VMEM((STEPS, 2, 256, LAT), BF),
            pltpu.VMEM((STEPS, 2, TP, 16, LAT), BF),
            pltpu.VMEM((STEPS, TP, 16, 128), BF),
            pltpu.VMEM((ROWS_DEV, HEADS, LAT), BF),
            pltpu.VMEM((ROWS_DEV, HEADS, 128), BF),
            pltpu.VMEM((2, ROWS_DEV, 16, LAT), BF),
            pltpu.VMEM((STEPS, 2, TP, 16, LAT), BF),
            pltpu.VMEM((STEPS, 2, 256, LAT), BF),
            pltpu.VMEM((STEPS, 256, 256), BF),
            pltpu.VMEM((STEPS, YS, 256, 256), BF),
            pltpu.VMEM((CHUNKS, YS, ZS, 16, HALF), BF),
            pltpu.VMEM((CHUNKS, 2, YS, 16, HALF), BF),
            pltpu.VMEM(chunk, BF),
            pltpu.VMEM(chunk, BF),
            pltpu.VMEM(chunk, BF),
            dma((8,)),
            dma((15,)),
            dma((REPS,)),
            dma((TP,)),
            dma((TP,)),
            dma(()),
            dma(()),
            dma((YS,)),
            dma((YS,)),
            dma((YS,)),
            dma((YS,)),
            dma((TP,)),
            dma((TP,)),
            dma((STEPS, TP)),
            dma((STEPS, TP)),
            dma((STEPS, TP)),
            dma((STEPS, TP)),
            dma((STEPS, YS)),
            dma((STEPS, YS)),
            dma((CHUNKS, 2)),
            dma((CHUNKS, 2)),
            dma((CHUNKS,)),
            dma((CHUNKS,)),
            dma((CHUNKS, YS)),
            dma((CHUNKS, YS)),
        ],
        compiler_params=pltpu.CompilerParams(
            collective_id=0, has_side_effects=True, vmem_limit_bytes=56 * 2**20
        ),
        name="push_and_decode",
    )(
        bucket_slot,
        bucket_version,
        replica_version,
        old_scale,
        lengths,
        trainer_weight,
        old_weight,
        q_nope,
        q_rope,
        cache_latent,
        cache_rope,
        new_token,
        out_weight,
    )


def solution(mesh):
    return jax.shard_map(
        local,
        mesh=mesh,
        in_specs=(
            P("rep", "tp", None),
            P(),
            P(),
            P("rep", None),
            P("rep", None, "tp"),
            P("rep", None, "tp"),
            P(None, "rep", None, "tp"),
            P(None, "rep", None, "tp"),
            P("rep", "tp", None, None),
            P("rep", "tp", None),
            P(None, "rep", "tp", None),
            P("rep", "tp"),
            P("tp", None),
        ),
        out_specs=(P("rep", None, "tp"), P("rep", None, "tp"), P(None, "rep", "tp", None)),
        check_vma=False,
    )
```

time: 414 us -> 126 us (0.30)
  waiting for transfers between devices: 169 us -> 0 us
  blocking collectives: 152 us -> 0 us
  Pallas kernels: 0 us -> 119 us
  matrix products: 22.2 us -> 0 us
  starting transfers between devices: 21.8 us -> 0 us
  local copies, waits for them, and re-layouts: 20.6 us -> 4.93 us
  between operations: 14.7 us -> 0.64 us
  other arithmetic: 13.1 us -> 0 us
    pallas_call x0 -> x1, Pallas kernels: none -> 119 us  [local(): pl.pallas_call(everything, out_shape=(jax.ShapeDtypeStruct((1, LAT, 512),...]
    reduce_scatter x2 -> x0, waiting for transfers between devices: 115 us -> none  [local(): lax.psum_scatter(projected(jnp.int32(0), rows_here * lax.axis_size('tp'))...]
    all_gather x2 -> x0, blocking collectives: 56.1 us -> none  [the longest x1 31.1 us: local(): lax.all_gather(bundle[1].astype(jnp.bfloat16), 'rep', axis=0, tiled=True)]
    all_to_all x5 -> x0, waiting for transfers between devices: 53.4 us -> none  [the longest x2 41.3 us: local(): lax.all_to_all(query_lat, 'tp', split_axis=0, concat_axis=1, tiled=True)]
    all_to_all x2 -> x0, blocking collectives: 50.6 us -> none  [local(): lax.all_to_all(attended, 'tp', split_axis=1, concat_axis=0, tiled=True)]
    pmax x1 -> x0, blocking collectives: 45 us -> none  [local(): block_peak = lax.pmax(own_peak, 'tp')]
    dot_general x18 -> x0, matrix products: 22.2 us -> none  [the longest x2 10.1 us: attend(): jnp.einsum('rhl,rjl->rhj', row_lat, keys_lat, preferred_element_type=jnp....]
    all_to_all x5 -> x0, starting transfers between devices: 21.6 us -> none  [the longest x2 10.9 us: local(): lax.all_to_all(query_rope, 'tp', split_axis=0, concat_axis=1, tiled=True)]
  transfers between devices with their start and end apart: 7 -> 0, of which waited for: 6 -> 0; matrix products, arithmetic and copies ran while one was open for 7% -> 0% of each run, Pallas kernels for 0% -> 0%
where the time goes in v2:
time: 126 us; the launch traced here: 125 us
  Pallas kernels  119 us (94%)
  local copies, waits for them, and re-layouts  4.93 us (4%)
    pallas_call x1, Pallas kernels, local(): pl.pallas_call(everything, out_shape=(jax.ShapeDtypeStruct((1, LAT, 512),...  119 us
    unnamed x3, local copies, waits for them, and re-layouts  4.93 us

profile of v2, /device:TPU:4, one launch (start us, length us, event | category | flops | bytes accessed | tf_op | source)
XLA Modules:
  0.0 125.0 jit_solution(15623952100116252931)
XLA Ops:
  0.6 119.4 %push_and_decode.1 = (bf16[1,512,512]{2,1,0:T(8,128)(2,1)}, f32[1,4,4]{2,1,0:T(4,128)}, bf16[2,1,16,7168]{3,2,1,0:T(8,128)(2,1)}) custom-call(s32[32]{0:T(128)} %slot_ref.1, s32[32]{0:T(128)} %bver_ref.1, s32[1,32]{1,0:T(1,128)} %rver_ref.1, f32[1,4,4]{2,1,0:T(4,128)} %oscale_ref.1, s32[1,16]{1,0:T(1,128)} %len_ref.1, bf16[2,32,256]{2,1,0:T(8,128)(2,1)} %tw_hbm.1, ...), custom_call_target="tpu_custom_call" | custom-call | tf_op jit(solution)/shard_map/push_and_decode/pallas_call | solution.py:549
  120.1 1.9 %copy.19 = bf16[1,512,512]{2,1,0:T(8,128)(2,1)} copy(bf16[1,512,512]{2,1,0:T(8,128)(2,1)} %get-tuple-element.6) | data formatting | bytes 1048576
  121.9 1.3 %copy.20 = f32[1,4,4]{2,1,0:T(4,128)} copy(f32[1,4,4]{2,1,0:T(4,128)} %get-tuple-element.7) | data formatting | bytes 128
  123.2 1.8 %copy.21 = bf16[2,1,16,7168]{3,2,1,0:T(8,128)(2,1)} copy(bf16[2,1,16,7168]{3,2,1,0:T(8,128)(2,1)} %get-tuple-element.8) | data formatting | bytes 917504

commit v3 on v2

v3 whole, which is shorter than its diff:
```python
import jax
import jax.numpy as jnp
from jax import lax
from jax.experimental import pallas as pl
from jax.experimental.pallas import tpu as pltpu
from jax.sharding import PartitionSpec as P

HEADS = 32
LAT = 512
NOPE = 128
ROPE = 64
VDIM = 128
BLOCK = 128
STEPS = 2
PARTS = 2
D = 7168
LEN = 384
YS = 4
ZS = 4
TP = YS * ZS
REPS = 16
ROWS_DEV = 16
COLS = D // YS
HALF = COLS // 2
CHUNKS = 4
EPSILON = 1e-06
SCALING = (NOPE + ROPE) ** (-0.5)
MESH = pl.DeviceIdType.MESH
BF = jnp.bfloat16
F32 = jnp.float32
VM = pl.BlockSpec(memory_space=pltpu.VMEM)
SM = pl.BlockSpec(memory_space=pltpu.SMEM)
ANY = pl.BlockSpec(memory_space=pl.ANY)


def rem(a, b):
    return lax.rem(a, jnp.int32(b))


def div(a, b):
    return lax.div(a, jnp.int32(b))


def rcopy(src, dst, send_sem, recv_sem, **where):
    return pltpu.make_async_remote_copy(
        src_ref=src,
        dst_ref=dst,
        send_sem=send_sem,
        recv_sem=recv_sem,
        device_id=where,
        device_id_type=MESH,
    )


def greet(peers):
    barrier = pltpu.get_barrier_semaphore()
    for peer in peers:
        pl.semaphore_signal(barrier, inc=1, device_id=peer, device_id_type=MESH)
    pl.semaphore_wait(barrier, len(peers))


def mm(a, b, contract=((1,), (0,))):
    return lax.dot_general(a, b, (contract, ((), ())), preferred_element_type=F32)


def everything(
    slot_ref,
    bver_ref,
    rver_ref,
    oscale_ref,
    len_ref,
    tw_hbm,
    ow_hbm,
    qn_hbm,
    qp_hbm,
    cache_hbm,
    rope_hbm,
    tok_hbm,
    weight_hbm,
    sw_ref,
    ss_ref,
    dec,
    gath,
    sel,
    buck,
    ow,
    km,
    vm,
    qn,
    qn2,
    rope,
    tok,
    cache,
    wp,
    perm,
    ropes,
    kr,
    toks,
    qs,
    qr,
    qrr,
    qrow,
    qro,
    attr,
    ab,
    ar,
    ho,
    hg,
    pb,
    r1,
    fin,
    hl,
    lsem,
    gsend,
    grecv,
    tsend,
    trecv,
    csend,
    crecv,
    wsend,
    wrecv,
    xsend,
    xrecv,
    dsend,
    drecv,
    esend,
    erecv,
    vsend,
    vrecv,
    psend,
    precv,
    qsend,
    qrecv,
    asend,
    arecv,
    hsend,
    hrecv,
    s1send,
    s1recv,
    fsend,
    frecv,
):
    rep, tp = lax.axis_index("rep"), lax.axis_index("tp")
    zh, x, c = div(rep, 8), rem(div(rep, 2), 4), rem(rep, 2)
    y, z = div(tp, ZS), rem(tp, ZS)
    zpeer = rem(rep + 8, 16)
    cpeer = rep + 1 - 2 * c
    xpeers = [zh * 8 + rem(x + dx, 4) * 2 + c for dx in (1, 2, 3)]
    near = z + 1 - 2 * rem(z, 2)
    far = rem(z + 2, ZS)
    side, par = div(z, 2), rem(z, 2)
    mine = 2 * y + par
    share = 2 * x + c

    def rows16(t):
        return pl.ds(pl.multiple_of(16 * t, 16), 16)

    def rows32(t):
        return pl.ds(pl.multiple_of(32 * t, 32), 32)

    def columns(yy):
        return pl.ds(pl.multiple_of(COLS * yy, 256), COLS)

    def each(fn):
        def body(k, carry):
            fn(k)
            return carry

        lax.fori_loop(1, TP, body, 0)

    def source(k):
        return rem(tp + TP - k, TP)

    def slot_at(owner, reader_side):
        oz = rem(owner, ZS)
        return 8 * rem(div(oz, 2) + reader_side, 2) + 2 * div(owner, ZS) + rem(oz, 2)

    def kin(j):
        m = rem(mine + j, 8)
        return m, div(m, 2) * ZS + 2 * side + rem(m, 2)

    def each_kin(fn):
        def body(j, carry):
            fn(j)
            return carry

        lax.fori_loop(1, 8, body, 0)

    loads = [
        pltpu.make_async_copy(src, dst, lsem.at[i])
        for i, (src, dst) in enumerate(
            [
                (tw_hbm, gath.at[pl.ds(2 * rep, 2)]),
                (qp_hbm.at[:, 0, rows16(tp), :], qrr.at[:, mine]),
                (tok_hbm.at[:, 0], tok),
                (rope_hbm.at[0], rope),
                (ow_hbm.at[0], ow),
                (qn_hbm.at[:, 0], qn),
                (cache_hbm.at[0], cache),
                (weight_hbm.at[:, columns(y)], wp.at[y, pl.ds(0, 256), :]),
            ]
        )
    ]
    load_tw, load_qp, load_tok, load_rope, load_ow, load_qn, load_cache, load_w = loads
    for copy in loads:
        copy.start()
    greet(
        [{"tp": rem(tp + k, TP)} for k in range(1, TP)]
        + [{"rep": r} for r in [zpeer, cpeer] + xpeers]
        + [{"rep": zpeer, "tp": yy * ZS + far} for yy in range(YS)]
    )

    def block(b):
        return gath.at[pl.ds(2 * b, 2)]

    sent = []

    def pass_on(src, b, to):
        copy = rcopy(src, block(b), gsend.at[len(sent)], grecv.at[b], rep=to)
        copy.start()
        sent.append(copy)

    def arrived(b):
        rcopy(block(b), block(b), gsend.at[0], grecv.at[b], rep=zpeer).wait_recv()

    def part(src):
        return buck.at[c, rows32(src), :]

    def pick_copy(k):
        t = rem(tp + k, TP)
        return rcopy(sel.at[k], part(tp), tsend.at[k], trecv.at[tp], tp=t)

    def half(yy, core):
        return wp.at[yy, pl.ds(pl.multiple_of(128 * core, 128), 128), :]

    def shared(yy, who):
        return wp.at[yy, pl.ds(pl.multiple_of(256 + 32 * who, 32), 32), :]

    def all_shared(who):
        return wp.at[:, pl.ds(pl.multiple_of(256 + 32 * who, 32), 32), :]

    def far_weight_copy(yy):
        src = weight_hbm.at[pl.ds(pl.multiple_of(32 * share, 32), 32), columns(yy)]
        to = rem(rep + 8 * (1 - c), 16)
        return rcopy(src, shared(y, share), dsend.at[yy], drecv.at[y], rep=to, tp=yy * ZS + far)

    def spread_copy(dx):
        to = xpeers[dx - 1]
        return rcopy(all_shared(share), all_shared(share), esend.at[dx], erecv.at[x], rep=to)

    def spread_swap(dx):
        who = 2 * rem(x + dx, 4) + c
        return rcopy(all_shared(who), all_shared(who), esend.at[4 + dx], erecv.at[4 + rem(x + dx, 4)], rep=cpeer)

    def value_copy():
        return rcopy(vm.at[0], vm.at[1], vsend, vrecv, tp=y * ZS + far)

    def weight_copy(dy):
        to = rem(y + dy, YS)
        src = weight_hbm.at[pl.ds(pl.multiple_of(128 * c, 128), 128), columns(to)]
        return rcopy(src, half(y, c), wsend.at[dy], wrecv.at[y], tp=to * ZS + z)

    def swap_copy(dy):
        src = rem(y + YS - dy, YS)
        return rcopy(half(src, c), half(src, c), xsend.at[dy], xrecv.at[src], rep=cpeer)

    def rope_copy(k):
        t = rem(tp + k, TP)
        there = qrr.at[:, slot_at(tp, div(rem(t, ZS), 2))]
        return rcopy(qp_hbm.at[:, 0, rows16(t), :], there, psend.at[k], precv.at[tp], tp=t)

    def query_copy(p, k):
        t = rem(tp + k, TP)
        there = qr.at[p, :, slot_at(tp, div(rem(t, ZS), 2))]
        return rcopy(qs.at[p, :, rows16(t), :], there, qsend.at[p, k], qrecv.at[p, tp], tp=t)

    def back_copy(p, j):
        m, t = kin(j)
        there = ar.at[p, :, :, rows16(mine), :]
        return rcopy(ab.at[p, :, :, m], there, asend.at[p, j], arecv.at[p, mine], tp=t)

    def gather_copy(p, dy):
        to = rem(y + dy, YS) * ZS + z
        return rcopy(ho.at[p], hg.at[p, y], hsend.at[p, dy], hrecv.at[p, y], tp=to)

    def near_copy(q):
        return rcopy(pb.at[q, :, 1 - par], r1.at[q], s1send.at[q], s1recv.at[q], tp=y * ZS + near)

    def home_copy(q, dy):
        to = rem(y + dy, YS)
        return rcopy(fin.at[q, to], hl.at[q, y], fsend.at[q, dy], frecv.at[q, y], tp=to * ZS + z)

    for to in [zpeer] + xpeers + [cpeer]:
        pass_on(tw_hbm, rep, to)
    weight_copy(1).start()
    weight_copy(3).start()
    arrived(zpeer)
    for to in xpeers + [cpeer]:
        pass_on(block(zpeer), zpeer, to)
    for yy in range(YS):
        far_weight_copy(yy).start()
    for xp in xpeers:
        arrived(xp)
        pass_on(block(xp), xp, cpeer)
    for xp in xpeers:
        b = rem(xp + 8, 16)
        arrived(b)
        pass_on(block(b), b, cpeer)
    load_tw.wait()
    for b in [cpeer, rem(cpeer + 8, 16)]:
        arrived(b)
    for xp in xpeers:
        other = xp + 1 - 2 * c
        arrived(other)
        arrived(rem(other + 8, 16))

    def pick(k):
        sel[k] = gath[slot_ref[2 * rem(tp + k, TP) + c]]
        pick_copy(k).start()

    each(pick)
    buck[c, rows32(tp), :] = gath[slot_ref[2 * tp + c]]
    each(lambda k: rope_copy(k).start())
    weight_copy(2).start()

    pi = lax.broadcasted_iota(jnp.int32, (256, 256), 0)
    pj = lax.broadcasted_iota(jnp.int32, (256, 256), 1)
    swapped = ((pi >> 4) == (pj & 15)) & ((pi & 15) == (pj >> 4))
    perm[...] = jnp.where(swapped, 1.0, 0.0).astype(BF)
    load_tok.wait()
    toks[...] = jnp.zeros_like(toks)
    toks[:, :, 0 : LAT + ROPE] = tok[...].astype(F32)
    load_rope.wait()
    for g in range(12):
        tiles = [rope[:, (16 * g + i) * 128 : (16 * g + i + 1) * 128] for i in range(16)]
        turned = mm(perm[...], jnp.concatenate(tiles, axis=0)).astype(BF)
        ropes[:, 16 * g : 16 * (g + 1), :] = turned.reshape(16, 16, 128)

    load_qn.wait()

    def reorder(t, carry):
        first = qn[0, rows16(t), :].astype(F32)
        second = qn[1, rows16(t), :].astype(F32)
        for p in range(PARTS):
            rows = slice(8 * p, 8 * p + 8)
            both = jnp.concatenate([first[rows], second[rows]], axis=0)
            qn2[p, rows16(t), :] = both.astype(BF)
        return carry

    lax.fori_loop(0, TP, reorder, 0)

    def bucket_arrived(k):
        src = source(k)
        rcopy(part(src), part(src), tsend.at[k], trecv.at[src], tp=src).wait_recv()

    each(bucket_arrived)
    swap = rcopy(buck.at[c], buck.at[c], csend, crecv, rep=cpeer)
    swap.start()
    load_ow.wait()
    rcopy(buck.at[1 - c], buck.at[1 - c], csend, crecv, rep=cpeer).wait_recv()

    cell_row = lax.broadcasted_iota(jnp.int32, (4, 4), 0)
    cell_col = lax.broadcasted_iota(jnp.int32, (4, 4), 1)

    def serve(hh, cc, scales):
        head = 2 * tp + hh
        stale = (rver_ref[0, head] != bver_ref[head]).astype(jnp.int32)
        col = hh * 256 + cc * BLOCK
        for i in range(4):
            rows = slice(i * BLOCK, (i + 1) * BLOCK)
            raw = buck[hh, rows, cc * BLOCK : (cc + 1) * BLOCK].astype(F32)
            peak = jnp.max(jnp.abs(raw), axis=0, keepdims=True)
            peak = jnp.max(peak, axis=1, keepdims=True)
            scale = peak + EPSILON
            fresh = (raw / scale).astype(BF).astype(F32)
            old = ow[rows, col : col + BLOCK].astype(F32)
            served = jnp.where(jnp.zeros((BLOCK, BLOCK), jnp.int32) + stale != 0, fresh, old)
            held = jnp.zeros((1, 1), F32) + oscale_ref[0, i, 2 * hh + cc]
            used = jnp.where(jnp.zeros((1, 1), jnp.int32) + stale != 0, scale, held)
            sw_ref[0, rows, col : col + BLOCK] = served.astype(BF)
            maps = km if cc == 0 else vm.at[0]
            maps[rows, hh * BLOCK : (hh + 1) * BLOCK] = (served * used).astype(BF)
            here = (cell_row == i) & (cell_col == 2 * hh + cc)
            scales = jnp.where(here, used, scales)
        return scales

    scales = jnp.zeros((4, 4), F32)
    for hh in range(2):
        scales = serve(hh, 0, scales)

    for p in range(PARTS):
        for hh in range(2):
            qs[p, hh] = mm(
                qn2[p, :, hh * NOPE : (hh + 1) * NOPE],
                km[:, hh * BLOCK : (hh + 1) * BLOCK],
                ((1,), (1,)),
            ).astype(BF)
        each(lambda k: query_copy(p, k).start())
    for hh in range(2):
        scales = serve(hh, 1, scales)
    ss_ref[0] = scales
    for p in range(PARTS):
        for hh in range(2):
            qr[p, hh, mine] = qs[p, hh, rows16(tp), :]
    for yy in range(YS):
        there = shared(yy, share)
        rcopy(there, there, dsend.at[yy], drecv.at[yy], tp=yy * ZS + far).wait_recv()
    for dx in (1, 2, 3):
        spread_copy(dx).start()
    spread_swap(0).start()

    si = lax.broadcasted_iota(jnp.int32, (LEN, LEN // 2), 0)
    sj = lax.broadcasted_iota(jnp.int32, (LEN, LEN // 2), 1)
    spread = jnp.where((si >> 1) == sj, 1.0, 0.0).astype(BF)
    ki = lax.broadcasted_iota(jnp.int32, (LEN, 128), 0)
    kj = lax.broadcasted_iota(jnp.int32, (LEN, 128), 1)
    kept = (ki & 1) == (kj >> 6)

    def place(r, carry):
        kr[r] = jnp.where(kept, mm(spread, ropes[r]), 0.0).astype(BF)
        return carry

    lax.fori_loop(0, ROWS_DEV, place, 0)
    load_cache.wait()
    load_qp.wait()

    di = lax.broadcasted_iota(jnp.int32, (128, 256), 0)
    dj = lax.broadcasted_iota(jnp.int32, (128, 256), 1)
    double = jnp.where(di == (dj >> 7) * 64 + (dj & 63), 1.0, 0.0).astype(BF)
    position = lax.broadcasted_iota(jnp.int32, (1, LEN), 1)

    def rope_arrived(k):
        src = source(k)
        there = qrr.at[:, slot_at(src, side)]
        rcopy(there, there, psend.at[k], precv.at[src], tp=src).wait_recv()

    each(rope_arrived)
    for s in range(STEPS):
        turned = mm(perm[...], qrr[s].reshape(256, 128)).astype(BF)
        turned = mm(turned, double).astype(BF)
        for hh in range(2):
            first = 16 * (2 * s + hh)
            qro[:, first : first + 16, :] = turned[:, 128 * hh : 128 * (hh + 1)].reshape(16, 16, 128)
    late = lax.broadcasted_iota(jnp.int32, (2 * HEADS, 1), 0) >= HEADS

    def weights_arrived():
        for dy in (1, 2, 3):
            src = rem(y + YS - dy, YS)
            there = half(src, c)
            rcopy(there, there, wsend.at[dy], wrecv.at[src], tp=src * ZS + z).wait_recv()
            swap_copy(dy).start()

    def spread_arrived():
        for dx in (1, 2, 3):
            xx = rem(x + dx, 4)
            there = all_shared(2 * xx + c)
            rcopy(there, there, esend.at[dx], erecv.at[xx], rep=cpeer).wait_recv()
            spread_swap(dx).start()

    def attend(p):
        def query_arrived(k):
            src = source(k)
            there = qr.at[p, :, slot_at(src, side)]
            rcopy(there, there, qsend.at[p, k], qrecv.at[p, src], tp=src).wait_recv()

        each(query_arrived)
        for hh in range(2):
            turned = mm(perm[...], qr[p, hh].reshape(256, LAT)).astype(BF)
            turned = turned.reshape(2, 8, 16, LAT)
            for s in range(STEPS):
                first = 16 * (2 * s + hh)
                qrow[:, first : first + 16, :] = turned[s]

        def attend_row(i, carry):
            r = 8 * p + i
            q_lat, q_rope, keys = qrow[i], qro[r], cache[r]
            score = mm(q_lat, keys, ((1,), (1,))) + mm(q_rope, kr[r], ((1,), (1,)))
            score = jnp.where(position < len_ref[0, r], score * SCALING, -jnp.inf)
            top = jnp.max(score, axis=1, keepdims=True)
            lat32, rope32 = q_lat.astype(F32), q_rope.astype(F32)
            news = []
            for t in range(STEPS):
                tok_r = toks[t, pl.ds(r, 1), :]
                new = jnp.sum(lat32 * tok_r[:, :LAT], axis=1, keepdims=True)
                new = new + jnp.sum(rope32 * tok_r[:, LAT:], axis=1, keepdims=True)
                new = new * SCALING
                if t == 1:
                    new = jnp.where(late, new, -jnp.inf)
                news.append((new, tok_r[:, :LAT]))
            for new, _ in news:
                top = jnp.maximum(top, new)
            expped = jnp.exp(score - top)
            new_exp = [jnp.exp(new - top) for new, _ in news]
            total = jnp.sum(expped, axis=1, keepdims=True)
            for e in new_exp:
                total = total + e
            inverse = 1.0 / total
            out = mm((expped * inverse).astype(BF), keys)
            for e, (_, tok_r) in zip(new_exp, news):
                out = out + (e * inverse).astype(BF).astype(F32) * tok_r
            out = out.astype(BF)
            for s in range(STEPS):
                for hh in range(2):
                    first = 16 * (2 * s + hh)
                    attr[hh, 8 * s + i] = out[first : first + 16]
            return carry

        lax.fori_loop(0, 8, attend_row, 0, unroll=4)
        for hh in range(2):
            turned = mm(perm[...], attr[hh].reshape(256, LAT)).astype(BF)
            ab[p, hh] = turned.reshape(2, 8, 16, LAT)
        each_kin(lambda j: back_copy(p, j).start())
        for hh in range(2):
            for f in range(2):
                ar[p, hh, f, rows16(mine), :] = ab[p, hh, f, mine]

    def heads_out(p):
        def back_arrived(j):
            m, t = kin(8 - j)
            there = ar.at[p, :, :, rows16(m), :]
            rcopy(there, there, asend.at[p, j], arecv.at[p, m], tp=t).wait_recv()

        each_kin(back_arrived)
        for f in range(2):
            for hh in range(2):
                first = 256 * f + VDIM * hh
                ho[p, :, first : first + VDIM] = mm(
                    ar[p, hh, f], vm[f, :, hh * VDIM : (hh + 1) * VDIM]
                ).astype(BF)
        for dy in (1, 2, 3):
            gather_copy(p, dy).start()
        hg[p, y] = ho[p]

    def multiply(p):
        for dy in (1, 2, 3):
            src = rem(y + YS - dy, YS)
            there = hg.at[p, src]
            rcopy(there, there, hsend.at[p, dy], hrecv.at[p, src], tp=src * ZS + z).wait_recv()
        for q in (2 * p, 2 * p + 1):
            for first, width in ((0, 512), (512, 384)):
                cols = slice(HALF * (q % 2) + first, HALF * (q % 2) + first + width)
                total = mm(hg[p, 0], wp[0, :, cols])
                for k in range(1, YS):
                    total = total + mm(hg[p, k], wp[k, :, cols])
                pb[q, :, :, :, first : first + width] = total.astype(BF).reshape(YS, 2, 16, width)
            near_copy(q).start()

    def finish(q):
        near_copy(q).wait_recv()
        fin[q] = (pb[q, :, par].astype(F32) + r1[q].astype(F32)).astype(BF)
        for dy in (1, 2, 3):
            home_copy(q, dy).start()
        hl[q, y] = fin[q, y]

    attend(0)
    value_copy().start()
    weights_arrived()
    attend(1)
    spread_arrived()
    value_copy().wait_recv()
    heads_out(0)
    load_w.wait()
    for dy in (1, 2, 3):
        src = rem(y + YS - dy, YS)
        there = half(src, 1 - c)
        rcopy(there, there, xsend.at[dy], xrecv.at[src], rep=cpeer).wait_recv()
    for xx in range(4):
        there = all_shared(2 * xx + 1 - c)
        rcopy(there, there, esend.at[4], erecv.at[4 + xx], rep=cpeer).wait_recv()
    multiply(0)
    heads_out(1)
    finish(0)
    multiply(1)
    finish(1)
    finish(2)
    finish(3)

    for q in range(CHUNKS):
        for dy in (1, 2, 3):
            src = rem(y + YS - dy, YS)
            there = hl.at[q, src]
            rcopy(there, there, fsend.at[q, dy], frecv.at[q, src], tp=src * ZS + z).wait_recv()
    for side_cols in range(2):
        for yy in range(YS):
            first = COLS * yy + HALF * side_cols
            top = hl[side_cols, yy].astype(F32)
            low = hl[2 + side_cols, yy].astype(F32)
            for s in range(STEPS):
                rows = slice(8 * s, 8 * s + 8)
                both = jnp.concatenate([top[rows], low[rows]], axis=0)
                dec[s, 0, :, first : first + HALF] = both.astype(BF)

    for copy in sent:
        copy.wait_send()
    each(lambda k: pick_copy(k).wait_send())
    swap.wait_send()
    each(lambda k: rope_copy(k).wait_send())
    for dy in (1, 2, 3):
        weight_copy(dy).wait_send()
        swap_copy(dy).wait_send()
    for yy in range(YS):
        far_weight_copy(yy).wait_send()
    for dx in range(4):
        if dx > 0:
            spread_copy(dx).wait_send()
        spread_swap(dx).wait_send()
    value_copy().wait_send()
    for p in range(PARTS):
        each(lambda k: query_copy(p, k).wait_send())
        each_kin(lambda j: back_copy(p, j).wait_send())
        for dy in (1, 2, 3):
            gather_copy(p, dy).wait_send()
    for q in range(CHUNKS):
        near_copy(q).wait_send()
        for dy in (1, 2, 3):
            home_copy(q, dy).wait_send()


def local(
    trainer_weight,
    bucket_slot,
    bucket_version,
    replica_version,
    old_weight,
    old_scale,
    q_nope,
    q_rope,
    cache_latent,
    cache_rope,
    new_token,
    lengths,
    out_weight,
):
    dma = pltpu.SemaphoreType.DMA
    chunk = (CHUNKS, YS, 16, HALF)
    return pl.pallas_call(
        everything,
        out_shape=(
            jax.ShapeDtypeStruct((1, LAT, 512), BF),
            jax.ShapeDtypeStruct((1, 4, 4), F32),
            jax.ShapeDtypeStruct((STEPS, 1, 16, D), BF),
        ),
        in_specs=[SM] * 5 + [ANY] * 8,
        out_specs=(VM, VM, VM),
        scratch_shapes=[
            pltpu.VMEM((HEADS, 32, 256), BF),
            pltpu.VMEM((TP, 32, 256), BF),
            pltpu.VMEM((2, LAT, 256), BF),
            pltpu.VMEM((LAT, 512), BF),
            pltpu.VMEM((LAT, 256), BF),
            pltpu.VMEM((2, LAT, 256), BF),
            pltpu.VMEM((STEPS, 256, 256), BF),
            pltpu.VMEM((PARTS, 256, 256), BF),
            pltpu.VMEM((ROWS_DEV, LEN * ROPE), BF),
            pltpu.VMEM((STEPS, ROWS_DEV, LAT + ROPE), BF),
            pltpu.VMEM((ROWS_DEV, LEN, LAT), BF),
            pltpu.VMEM((YS, 512, COLS), BF),
            pltpu.VMEM((256, 256), BF),
            pltpu.VMEM((ROWS_DEV, LEN // 2, 128), BF),
            pltpu.VMEM((ROWS_DEV, LEN, 128), BF),
            pltpu.VMEM((STEPS, ROWS_DEV, 640), F32),
            pltpu.VMEM((PARTS, 2, 256, LAT), BF),
            pltpu.VMEM((PARTS, 2, TP, 16, LAT), BF),
            pltpu.VMEM((STEPS, TP, 16, 128), BF),
            pltpu.VMEM((8, 2 * HEADS, LAT), BF),
            pltpu.VMEM((ROWS_DEV, 2 * HEADS, 128), BF),
            pltpu.VMEM((2, 16, 16, LAT), BF),
            pltpu.VMEM((PARTS, 2, 2, 8, 16, LAT), BF),
            pltpu.VMEM((PARTS, 2, 2, 128, LAT), BF),
            pltpu.VMEM((PARTS, 128, 512), BF),
            pltpu.VMEM((PARTS, YS, 128, 512), BF),
            pltpu.VMEM((CHUNKS, YS, 2, 16, HALF), BF),
            pltpu.VMEM(chunk, BF),
            pltpu.VMEM(chunk, BF),
            pltpu.VMEM(chunk, BF),
            dma((8,)),
            dma((15,)),
            dma((REPS,)),
            dma((TP,)),
            dma((TP,)),
            dma(()),
            dma(()),
            dma((YS,)),
            dma((YS,)),
            dma((YS,)),
            dma((YS,)),
            dma((YS,)),
            dma((YS,)),
            dma((8,)),
            dma((8,)),
            dma(()),
            dma(()),
            dma((TP,)),
            dma((TP,)),
            dma((PARTS, TP)),
            dma((PARTS, TP)),
            dma((PARTS, 8)),
            dma((PARTS, 8)),
            dma((PARTS, YS)),
            dma((PARTS, YS)),
            dma((CHUNKS,)),
            dma((CHUNKS,)),
            dma((CHUNKS, YS)),
            dma((CHUNKS, YS)),
        ],
        compiler_params=pltpu.CompilerParams(
            collective_id=0, has_side_effects=True, vmem_limit_bytes=56 * 2**20
        ),
        name="push_and_decode",
    )(
        bucket_slot,
        bucket_version,
        replica_version,
        old_scale,
        lengths,
        trainer_weight,
        old_weight,
        q_nope,
        q_rope,
        cache_latent,
        cache_rope,
        new_token,
        out_weight,
    )


def solution(mesh):
    return jax.shard_map(
        local,
        mesh=mesh,
        in_specs=(
            P("rep", "tp", None),
            P(),
            P(),
            P("rep", None),
            P("rep", None, "tp"),
            P("rep", None, "tp"),
            P(None, "rep", None, "tp"),
            P(None, "rep", None, "tp"),
            P("rep", "tp", None, None),
            P("rep", "tp", None),
            P(None, "rep", "tp", None),
            P("rep", "tp"),
            P("tp", None),
        ),
        out_specs=(P("rep", None, "tp"), P("rep", None, "tp"), P(None, "rep", "tp", None)),
        check_vma=False,
    )
```

time: 126 us -> 113 us (0.90)
  the two profiles are of different devices: /device:TPU:4 before, /device:TPU:128 now
where the time goes in v3:
time: 113 us; the launch traced here: 112 us
  Pallas kernels  107 us (95%)
  local copies, waits for them, and re-layouts  4.93 us (4%)
    pallas_call x1, Pallas kernels, local(): pl.pallas_call(everything, out_shape=(jax.ShapeDtypeStruct((1, LAT, 512),...  107 us
    unnamed x3, local copies, waits for them, and re-layouts  4.93 us

profile of v3, /device:TPU:128, one launch (start us, length us, event | category | flops | bytes accessed | tf_op | source)
XLA Modules:
  0.0 112.4 jit_solution(16517139716020843271)
XLA Ops:
  0.6 106.9 %push_and_decode.1 = (bf16[1,512,512]{2,1,0:T(8,128)(2,1)}, f32[1,4,4]{2,1,0:T(4,128)}, bf16[2,1,16,7168]{3,2,1,0:T(8,128)(2,1)}) custom-call(s32[32]{0:T(128)} %slot_ref.1, s32[32]{0:T(128)} %bver_ref.1, s32[1,32]{1,0:T(1,128)} %rver_ref.1, f32[1,4,4]{2,1,0:T(4,128)} %oscale_ref.1, s32[1,16]{1,0:T(1,128)} %len_ref.1, bf16[2,32,256]{2,1,0:T(8,128)(2,1)} %tw_hbm.1, ...), custom_call_target="tpu_custom_call" | custom-call | tf_op jit(solution)/shard_map/push_and_decode/pallas_call | solution.py:636
  107.5 1.9 %copy.19 = bf16[1,512,512]{2,1,0:T(8,128)(2,1)} copy(bf16[1,512,512]{2,1,0:T(8,128)(2,1)} %get-tuple-element.6) | data formatting | bytes 1048576
  109.4 1.3 %copy.20 = f32[1,4,4]{2,1,0:T(4,128)} copy(f32[1,4,4]{2,1,0:T(4,128)} %get-tuple-element.7) | data formatting | bytes 128
  110.6 1.8 %copy.21 = bf16[2,1,16,7168]{3,2,1,0:T(8,128)(2,1)} copy(bf16[2,1,16,7168]{3,2,1,0:T(8,128)(2,1)} %get-tuple-element.8) | data formatting | bytes 917504

commit v4 on v3

--- a/solution.py
+++ b/solution.py
@@ -30,7 +30,7 @@
 F32 = jnp.float32
 VM = pl.BlockSpec(memory_space=pltpu.VMEM)
 SM = pl.BlockSpec(memory_space=pltpu.SMEM)
-ANY = pl.BlockSpec(memory_space=pl.ANY)
+HB = pl.BlockSpec(memory_space=pltpu.HBM)
 
 
 def rem(a, b):
@@ -107,8 +107,6 @@
     ho,
     hg,
     pb,
-    r1,
-    fin,
     hl,
     lsem,
     gsend,
@@ -123,8 +121,6 @@
     xrecv,
     dsend,
     drecv,
-    esend,
-    erecv,
     vsend,
     vrecv,
     psend,
@@ -135,8 +131,6 @@
     arecv,
     hsend,
     hrecv,
-    s1send,
-    s1recv,
     fsend,
     frecv,
 ):
@@ -146,7 +140,6 @@
     zpeer = rem(rep + 8, 16)
     cpeer = rep + 1 - 2 * c
     xpeers = [zh * 8 + rem(x + dx, 4) * 2 + c for dx in (1, 2, 3)]
-    near = z + 1 - 2 * rem(z, 2)
     far = rem(z + 2, ZS)
     side, par = div(z, 2), rem(z, 2)
     mine = 2 * y + par
@@ -197,7 +190,7 @@
                 (ow_hbm.at[0], ow),
                 (qn_hbm.at[:, 0], qn),
                 (cache_hbm.at[0], cache),
-                (weight_hbm.at[:, columns(y)], wp.at[y, pl.ds(0, 256), :]),
+                (weight_hbm.at[:, columns(y)], wp.at[0, pl.ds(0, 256), :]),
             ]
         )
     ]
@@ -206,7 +199,7 @@
         copy.start()
     greet(
         [{"tp": rem(tp + k, TP)} for k in range(1, TP)]
-        + [{"rep": r} for r in [zpeer, cpeer] + xpeers]
+        + [{"rep": r} for r in xpeers + [zpeer, cpeer]]
         + [{"rep": zpeer, "tp": yy * ZS + far} for yy in range(YS)]
     )
 
@@ -230,39 +223,57 @@
         t = rem(tp + k, TP)
         return rcopy(sel.at[k], part(tp), tsend.at[k], trecv.at[tp], tp=t)
 
-    def half(yy, core):
-        return wp.at[yy, pl.ds(pl.multiple_of(128 * core, 128), 128), :]
-
-    def shared(yy, who):
-        return wp.at[yy, pl.ds(pl.multiple_of(256 + 32 * who, 32), 32), :]
-
-    def all_shared(who):
-        return wp.at[:, pl.ds(pl.multiple_of(256 + 32 * who, 32), 32), :]
-
-    def far_weight_copy(yy):
-        src = weight_hbm.at[pl.ds(pl.multiple_of(32 * share, 32), 32), columns(yy)]
+    def swap_bucket():
+        return rcopy(buck.at[c], buck.at[c], csend, crecv, rep=cpeer)
+
+    def eighth(f, who):
+        return pl.ds(pl.multiple_of(256 * f + 32 * who, 32), 32)
+
+    def eighths(f, who):
+        return wp.at[pl.ds(1 - f, 3 + f), eighth(f, who), :]
+
+    own_eighth = pl.ds(pl.multiple_of(32 * share, 32), 32)
+
+    def weight_copy(f, dy):
+        yy = rem(y + dy, YS)
+        src = weight_hbm.at[own_eighth, columns(yy)]
+        there = wp.at[(YS - dy) % YS, eighth(f, share), :]
+        if f == 0:
+            return rcopy(src, there, wsend.at[f, dy], wrecv.at[f, (YS - dy) % YS], tp=yy * ZS + z)
         to = rem(rep + 8 * (1 - c), 16)
-        return rcopy(src, shared(y, share), dsend.at[yy], drecv.at[y], rep=to, tp=yy * ZS + far)
-
-    def spread_copy(dx):
-        to = xpeers[dx - 1]
-        return rcopy(all_shared(share), all_shared(share), esend.at[dx], erecv.at[x], rep=to)
-
-    def spread_swap(dx):
-        who = 2 * rem(x + dx, 4) + c
-        return rcopy(all_shared(who), all_shared(who), esend.at[4 + dx], erecv.at[4 + rem(x + dx, 4)], rep=cpeer)
+        return rcopy(src, there, wsend.at[f, dy], wrecv.at[f, (YS - dy) % YS], rep=to, tp=yy * ZS + far)
+
+    def spread_copy(f, dx):
+        here = eighths(f, share)
+        return rcopy(here, here, xsend.at[f, dx], xrecv.at[f, x], rep=xpeers[dx - 1])
+
+    def core_copy(f, dx):
+        xx = rem(x + dx, 4)
+        here = eighths(f, 2 * xx + c)
+        return rcopy(here, here, dsend.at[f, dx], drecv.at[f, xx], rep=cpeer)
+
+    def spread_weights(f):
+        for j in range(1 - f, YS):
+            there = wp.at[j, eighth(f, share), :]
+            rcopy(there, there, wsend.at[f, j], wrecv.at[f, j], rep=cpeer).wait_recv()
+        for dx in (2, 1, 3):
+            spread_copy(f, dx).start()
+        core_copy(f, 0).start()
+
+    def share_weights(f):
+        for dx in (1, 3, 2):
+            xx = rem(x + dx, 4)
+            there = eighths(f, 2 * xx + c)
+            rcopy(there, there, xsend.at[f, dx], xrecv.at[f, xx], rep=cpeer).wait_recv()
+            core_copy(f, dx).start()
+
+    def weights_arrived(f):
+        for xx in range(4):
+            there = eighths(f, 2 * xx + 1 - c)
+            rcopy(there, there, dsend.at[f, 0], drecv.at[f, xx], rep=cpeer).wait_recv()
 
     def value_copy():
         return rcopy(vm.at[0], vm.at[1], vsend, vrecv, tp=y * ZS + far)
-
-    def weight_copy(dy):
-        to = rem(y + dy, YS)
-        src = weight_hbm.at[pl.ds(pl.multiple_of(128 * c, 128), 128), columns(to)]
-        return rcopy(src, half(y, c), wsend.at[dy], wrecv.at[y], tp=to * ZS + z)
-
-    def swap_copy(dy):
-        src = rem(y + YS - dy, YS)
-        return rcopy(half(src, c), half(src, c), xsend.at[dy], xrecv.at[src], rep=cpeer)
 
     def rope_copy(k):
         t = rem(tp + k, TP)
@@ -281,24 +292,22 @@
 
     def gather_copy(p, dy):
         to = rem(y + dy, YS) * ZS + z
-        return rcopy(ho.at[p], hg.at[p, y], hsend.at[p, dy], hrecv.at[p, y], tp=to)
-
-    def near_copy(q):
-        return rcopy(pb.at[q, :, 1 - par], r1.at[q], s1send.at[q], s1recv.at[q], tp=y * ZS + near)
-
-    def home_copy(q, dy):
-        to = rem(y + dy, YS)
-        return rcopy(fin.at[q, to], hl.at[q, y], fsend.at[q, dy], frecv.at[q, y], tp=to * ZS + z)
+        return rcopy(ho.at[p], hg.at[p, YS - dy], hsend.at[p, dy], hrecv.at[p, YS - dy], tp=to)
+
+    def home_copy(q, j):
+        m, t = kin(j)
+        there = hl.at[q, y, par]
+        return rcopy(pb.at[q, div(m, 2), rem(m, 2)], there, fsend.at[q, j], frecv.at[q, mine], tp=t)
 
     for to in [zpeer] + xpeers + [cpeer]:
         pass_on(tw_hbm, rep, to)
-    weight_copy(1).start()
-    weight_copy(3).start()
+    for dy in (2, 1, 3):
+        weight_copy(0, dy).start()
     arrived(zpeer)
     for to in xpeers + [cpeer]:
         pass_on(block(zpeer), zpeer, to)
-    for yy in range(YS):
-        far_weight_copy(yy).start()
+    for dy in range(YS):
+        weight_copy(1, dy).start()
     for xp in xpeers:
         arrived(xp)
         pass_on(block(xp), xp, cpeer)
@@ -307,12 +316,8 @@
         arrived(b)
         pass_on(block(b), b, cpeer)
     load_tw.wait()
-    for b in [cpeer, rem(cpeer + 8, 16)]:
-        arrived(b)
-    for xp in xpeers:
-        other = xp + 1 - 2 * c
-        arrived(other)
-        arrived(rem(other + 8, 16))
+    for b in [zpeer, rep] + xpeers + [rem(xp + 8, 16) for xp in xpeers]:
+        arrived(b + 1 - 2 * c)
 
     def pick(k):
         sel[k] = gath[slot_ref[2 * rem(tp + k, TP) + c]]
@@ -320,8 +325,8 @@
 
     each(pick)
     buck[c, rows32(tp), :] = gath[slot_ref[2 * tp + c]]
+    spread_weights(0)
     each(lambda k: rope_copy(k).start())
-    weight_copy(2).start()
 
     pi = lax.broadcasted_iota(jnp.int32, (256, 256), 0)
     pj = lax.broadcasted_iota(jnp.int32, (256, 256), 1)
@@ -349,15 +354,16 @@
 
     lax.fori_loop(0, TP, reorder, 0)
 
+    load_ow.wait()
+
     def bucket_arrived(k):
         src = source(k)
         rcopy(part(src), part(src), tsend.at[k], trecv.at[src], tp=src).wait_recv()
 
     each(bucket_arrived)
-    swap = rcopy(buck.at[c], buck.at[c], csend, crecv, rep=cpeer)
-    swap.start()
-    load_ow.wait()
-    rcopy(buck.at[1 - c], buck.at[1 - c], csend, crecv, rep=cpeer).wait_recv()
+    swap_bucket().start()
+    there = buck.at[1 - c]
+    rcopy(there, there, csend, crecv, rep=cpeer).wait_recv()
 
     cell_row = lax.broadcasted_iota(jnp.int32, (4, 4), 0)
     cell_col = lax.broadcasted_iota(jnp.int32, (4, 4), 1)
@@ -396,18 +402,13 @@
                 ((1,), (1,)),
             ).astype(BF)
         each(lambda k: query_copy(p, k).start())
+    spread_weights(1)
     for hh in range(2):
         scales = serve(hh, 1, scales)
     ss_ref[0] = scales
     for p in range(PARTS):
         for hh in range(2):
             qr[p, hh, mine] = qs[p, hh, rows16(tp), :]
-    for yy in range(YS):
-        there = shared(yy, share)
-        rcopy(there, there, dsend.at[yy], drecv.at[yy], tp=yy * ZS + far).wait_recv()
-    for dx in (1, 2, 3):
-        spread_copy(dx).start()
-    spread_swap(0).start()
 
     si = lax.broadcasted_iota(jnp.int32, (LEN, LEN // 2), 0)
     sj = lax.broadcasted_iota(jnp.int32, (LEN, LEN // 2), 1)
@@ -442,20 +443,6 @@
             first = 16 * (2 * s + hh)
             qro[:, first : first + 16, :] = turned[:, 128 * hh : 128 * (hh + 1)].reshape(16, 16, 128)
     late = lax.broadcasted_iota(jnp.int32, (2 * HEADS, 1), 0) >= HEADS
-
-    def weights_arrived():
-        for dy in (1, 2, 3):
-            src = rem(y + YS - dy, YS)
-            there = half(src, c)
-            rcopy(there, there, wsend.at[dy], wrecv.at[src], tp=src * ZS + z).wait_recv()
-            swap_copy(dy).start()
-
-    def spread_arrived():
-        for dx in (1, 2, 3):
-            xx = rem(x + dx, 4)
-            there = all_shared(2 * xx + c)
-            rcopy(there, there, esend.at[dx], erecv.at[xx], rep=cpeer).wait_recv()
-            spread_swap(dx).start()
 
     def attend(p):
         def query_arrived(k):
@@ -529,13 +516,13 @@
                 ).astype(BF)
         for dy in (1, 2, 3):
             gather_copy(p, dy).start()
-        hg[p, y] = ho[p]
+        hg[p, 0] = ho[p]
 
     def multiply(p):
         for dy in (1, 2, 3):
-            src = rem(y + YS - dy, YS)
-            there = hg.at[p, src]
-            rcopy(there, there, hsend.at[p, dy], hrecv.at[p, src], tp=src * ZS + z).wait_recv()
+            src = rem(y + dy, YS)
+            there = hg.at[p, dy]
+            rcopy(there, there, hsend.at[p, dy], hrecv.at[p, dy], tp=src * ZS + z).wait_recv()
         for q in (2 * p, 2 * p + 1):
             for first, width in ((0, 512), (512, 384)):
                 cols = slice(HALF * (q % 2) + first, HALF * (q % 2) + first + width)
@@ -543,48 +530,36 @@
                 for k in range(1, YS):
                     total = total + mm(hg[p, k], wp[k, :, cols])
                 pb[q, :, :, :, first : first + width] = total.astype(BF).reshape(YS, 2, 16, width)
-            near_copy(q).start()
-
-    def finish(q):
-        near_copy(q).wait_recv()
-        fin[q] = (pb[q, :, par].astype(F32) + r1[q].astype(F32)).astype(BF)
-        for dy in (1, 2, 3):
-            home_copy(q, dy).start()
-        hl[q, y] = fin[q, y]
+            each_kin(lambda j: home_copy(q, j).start())
+            hl[q, y, par] = pb[q, y, par]
+
+    def home_arrived(q, j):
+        m, t = kin(8 - j)
+        there = hl.at[q, div(m, 2), rem(m, 2)]
+        rcopy(there, there, fsend.at[q, j], frecv.at[q, m], tp=t).wait_recv()
 
     attend(0)
     value_copy().start()
-    weights_arrived()
+    share_weights(0)
     attend(1)
-    spread_arrived()
+    share_weights(1)
     value_copy().wait_recv()
     heads_out(0)
+    heads_out(1)
     load_w.wait()
-    for dy in (1, 2, 3):
-        src = rem(y + YS - dy, YS)
-        there = half(src, 1 - c)
-        rcopy(there, there, xsend.at[dy], xrecv.at[src], rep=cpeer).wait_recv()
-    for xx in range(4):
-        there = all_shared(2 * xx + 1 - c)
-        rcopy(there, there, esend.at[4], erecv.at[4 + xx], rep=cpeer).wait_recv()
+    for f in range(2):
+        weights_arrived(f)
     multiply(0)
-    heads_out(1)
-    finish(0)
     multiply(1)
-    finish(1)
-    finish(2)
-    finish(3)
 
     for q in range(CHUNKS):
-        for dy in (1, 2, 3):
-            src = rem(y + YS - dy, YS)
-            there = hl.at[q, src]
-            rcopy(there, there, fsend.at[q, dy], frecv.at[q, src], tp=src * ZS + z).wait_recv()
+        each_kin(lambda j: home_arrived(q, j))
     for side_cols in range(2):
         for yy in range(YS):
             first = COLS * yy + HALF * side_cols
-            top = hl[side_cols, yy].astype(F32)
-            low = hl[2 + side_cols, yy].astype(F32)
+            top, low = (
+                hl[q, yy, 0].astype(F32) + hl[q, yy, 1].astype(F32) for q in (side_cols, 2 + side_cols)
+            )
             for s in range(STEPS):
                 rows = slice(8 * s, 8 * s + 8)
                 both = jnp.concatenate([top[rows], low[rows]], axis=0)
@@ -593,17 +568,15 @@
     for copy in sent:
         copy.wait_send()
     each(lambda k: pick_copy(k).wait_send())
-    swap.wait_send()
+    swap_bucket().wait_send()
     each(lambda k: rope_copy(k).wait_send())
-    for dy in (1, 2, 3):
-        weight_copy(dy).wait_send()
-        swap_copy(dy).wait_send()
-    for yy in range(YS):
-        far_weight_copy(yy).wait_send()
-    for dx in range(4):
-        if dx > 0:
-            spread_copy(dx).wait_send()
-        spread_swap(dx).wait_send()
+    for f in range(2):
+        for dy in range(1 - f, YS):
+            weight_copy(f, dy).wait_send()
+        for dx in range(4):
+            if dx > 0:
+                spread_copy(f, dx).wait_send()
+            core_copy(f, dx).wait_send()
     value_copy().wait_send()
     for p in range(PARTS):
         each(lambda k: query_copy(p, k).wait_send())
@@ -611,9 +584,12 @@
         for dy in (1, 2, 3):
             gather_copy(p, dy).wait_send()
     for q in range(CHUNKS):
-        near_copy(q).wait_send()
-        for dy in (1, 2, 3):
-            home_copy(q, dy).wait_send()
+        each_kin(lambda j: home_copy(q, j).wait_send())
+
+
+def hand_over(*refs):
+    for source, result in zip(refs[:3], refs[3:]):
+        result[...] = source[...]
 
 
 def local(
@@ -632,15 +608,14 @@
     out_weight,
 ):
     dma = pltpu.SemaphoreType.DMA
-    chunk = (CHUNKS, YS, 16, HALF)
-    return pl.pallas_call(
+    results = pl.pallas_call(
         everything,
         out_shape=(
             jax.ShapeDtypeStruct((1, LAT, 512), BF),
             jax.ShapeDtypeStruct((1, 4, 4), F32),
             jax.ShapeDtypeStruct((STEPS, 1, 16, D), BF),
         ),
-        in_specs=[SM] * 5 + [ANY] * 8,
+        in_specs=[SM] * 5 + [HB] * 8,
         out_specs=(VM, VM, VM),
         scratch_shapes=[
             pltpu.VMEM((HEADS, 32, 256), BF),
@@ -670,9 +645,7 @@
             pltpu.VMEM((PARTS, 128, 512), BF),
             pltpu.VMEM((PARTS, YS, 128, 512), BF),
             pltpu.VMEM((CHUNKS, YS, 2, 16, HALF), BF),
-            pltpu.VMEM(chunk, BF),
-            pltpu.VMEM(chunk, BF),
-            pltpu.VMEM(chunk, BF),
+            pltpu.VMEM((CHUNKS, YS, 2, 16, HALF), BF),
             dma((8,)),
             dma((15,)),
             dma((REPS,)),
@@ -680,14 +653,12 @@
             dma((TP,)),
             dma(()),
             dma(()),
-            dma((YS,)),
-            dma((YS,)),
-            dma((YS,)),
-            dma((YS,)),
-            dma((YS,)),
-            dma((YS,)),
-            dma((8,)),
-            dma((8,)),
+            dma((2, YS)),
+            dma((2, YS)),
+            dma((2, 4)),
+            dma((2, 4)),
+            dma((2, 4)),
+            dma((2, 4)),
             dma(()),
             dma(()),
             dma((TP,)),
@@ -698,10 +669,8 @@
             dma((PARTS, 8)),
             dma((PARTS, YS)),
             dma((PARTS, YS)),
-            dma((CHUNKS,)),
-            dma((CHUNKS,)),
-            dma((CHUNKS, YS)),
-            dma((CHUNKS, YS)),
+            dma((CHUNKS, 8)),
+            dma((CHUNKS, 8)),
         ],
         compiler_params=pltpu.CompilerParams(
             collective_id=0, has_side_effects=True, vmem_limit_bytes=56 * 2**20
@@ -722,6 +691,14 @@
         new_token,
         out_weight,
     )
+    return pl.pallas_call(
+        hand_over,
+        out_shape=tuple(jax.ShapeDtypeStruct(r.shape, r.dtype) for r in results),
+        in_specs=[VM] * 3,
+        out_specs=(VM,) * 3,
+        compiler_params=pltpu.CompilerParams(vmem_limit_bytes=56 * 2**20),
+        name="hand_over",
+    )(*results)
 
 
 def solution(mesh):

time: 113 us -> 106 us (0.938)
  the two profiles are of different devices: /device:TPU:128 before, /device:TPU:4 now
where the time goes in v4:
time: 106 us; the launch traced here: 105 us
  Pallas kernels  104 us (98%)
    pallas_call x1, Pallas kernels, local(): pl.pallas_call(everything, out_shape=(jax.ShapeDtypeStruct((1, LAT, 512),...  102 us
    pallas_call x1, Pallas kernels, local(): pl.pallas_call(hand_over, out_shape=tuple((jax.ShapeDtypeStruct(r.shape,...  2.16 us

profile of v4, /device:TPU:4, one launch (start us, length us, event | category | flops | bytes accessed | tf_op | source)
XLA Modules:
  0.0 104.6 jit_solution(7393862746647435064)
XLA Ops:
  0.6 101.8 %push_and_decode.1 = (bf16[1,512,512]{2,1,0:T(8,128)(2,1)}, f32[1,4,4]{2,1,0:T(4,128)}, bf16[2,1,16,7168]{3,2,1,0:T(8,128)(2,1)}) custom-call(s32[32]{0:T(128)} %slot_ref.1, s32[32]{0:T(128)} %bver_ref.1, s32[1,32]{1,0:T(1,128)} %rver_ref.1, f32[1,4,4]{2,1,0:T(4,128)} %oscale_ref.1, s32[1,16]{1,0:T(1,128)} %len_ref.1, bf16[2,32,256]{2,1,0:T(8,128)(2,1)} %tw_hbm.1, ...), custom_call_target="tpu_custom_call" | custom-call | tf_op jit(solution)/shard_map/push_and_decode/pallas_call | solution.py:611
  102.4 2.2 %hand_over.1 = (bf16[1,512,512]{2,1,0:T(8,128)(2,1)}, f32[1,4,4]{2,1,0:T(4,128)}, bf16[2,1,16,7168]{3,2,1,0:T(8,128)(2,1)}) custom-call(bf16[1,512,512]{2,1,0:T(8,128)(2,1)} %get-tuple-element.6.refs_0_, f32[1,4,4]{2,1,0:T(4,128)} %get-tuple-element.7.refs_1_, bf16[2,1,16,7168]{3,2,1,0:T(8,128)(2,1)} %get-tuple-element.8.refs_2_), custom_call_target="tpu_custom_call" | custom-call | tf_op jit(solution)/shard_map/hand_over/pallas_call | solution.py:694

commit v5 on v4

--- a/solution.py
+++ b/solution.py
@@ -301,13 +301,13 @@
 
     for to in [zpeer] + xpeers + [cpeer]:
         pass_on(tw_hbm, rep, to)
-    for dy in (2, 1, 3):
-        weight_copy(0, dy).start()
+    for dy in range(YS):
+        weight_copy(1, dy).start()
     arrived(zpeer)
     for to in xpeers + [cpeer]:
         pass_on(block(zpeer), zpeer, to)
-    for dy in range(YS):
-        weight_copy(1, dy).start()
+    for dy in (2, 1, 3):
+        weight_copy(0, dy).start()
     for xp in xpeers:
         arrived(xp)
         pass_on(block(xp), xp, cpeer)

time: 106 us -> 101 us (0.953)
  Pallas kernels: 104 us -> 99.2 us
    pallas_call x1, Pallas kernels: 102 us -> 97.1 us  [local(): pl.pallas_call(everything, out_shape=(jax.ShapeDtypeStruct((1, LAT, 512),...]
where the time goes in v5:
time: 101 us; the launch traced here: 99.9 us
  Pallas kernels  99.2 us (98%)
    pallas_call x1, Pallas kernels, local(): pl.pallas_call(everything, out_shape=(jax.ShapeDtypeStruct((1, LAT, 512),...  97.1 us
    pallas_call x1, Pallas kernels, local(): pl.pallas_call(hand_over, out_shape=tuple((jax.ShapeDtypeStruct(r.shape,...  2.16 us

profile of v5, /device:TPU:4, one launch (start us, length us, event | category | flops | bytes accessed | tf_op | source)
XLA Modules:
  0.0 99.9 jit_solution(904617387442351216)
XLA Ops:
  0.6 97.1 %push_and_decode.1 = (bf16[1,512,512]{2,1,0:T(8,128)(2,1)}, f32[1,4,4]{2,1,0:T(4,128)}, bf16[2,1,16,7168]{3,2,1,0:T(8,128)(2,1)}) custom-call(s32[32]{0:T(128)} %slot_ref.1, s32[32]{0:T(128)} %bver_ref.1, s32[1,32]{1,0:T(1,128)} %rver_ref.1, f32[1,4,4]{2,1,0:T(4,128)} %oscale_ref.1, s32[1,16]{1,0:T(1,128)} %len_ref.1, bf16[2,32,256]{2,1,0:T(8,128)(2,1)} %tw_hbm.1, ...), custom_call_target="tpu_custom_call" | custom-call | tf_op jit(solution)/shard_map/push_and_decode/pallas_call | solution.py:611
  97.7 2.2 %hand_over.1 = (bf16[1,512,512]{2,1,0:T(8,128)(2,1)}, f32[1,4,4]{2,1,0:T(4,128)}, bf16[2,1,16,7168]{3,2,1,0:T(8,128)(2,1)}) custom-call(bf16[1,512,512]{2,1,0:T(8,128)(2,1)} %get-tuple-element.6.refs_0_, f32[1,4,4]{2,1,0:T(4,128)} %get-tuple-element.7.refs_1_, bf16[2,1,16,7168]{3,2,1,0:T(8,128)(2,1)} %get-tuple-element.8.refs_2_), custom_call_target="tpu_custom_call" | custom-call | tf_op jit(solution)/shard_map/hand_over/pallas_call | solution.py:694

commit v6 on v5

--- a/solution.py
+++ b/solution.py
@@ -77,9 +77,10 @@
     rope_hbm,
     tok_hbm,
     weight_hbm,
-    sw_ref,
+    sw_hbm,
     ss_ref,
     dec,
+    served_now,
     gath,
     sel,
     buck,
@@ -383,7 +384,7 @@
             served = jnp.where(jnp.zeros((BLOCK, BLOCK), jnp.int32) + stale != 0, fresh, old)
             held = jnp.zeros((1, 1), F32) + oscale_ref[0, i, 2 * hh + cc]
             used = jnp.where(jnp.zeros((1, 1), jnp.int32) + stale != 0, scale, held)
-            sw_ref[0, rows, col : col + BLOCK] = served.astype(BF)
+            served_now[rows, col : col + BLOCK] = served.astype(BF)
             maps = km if cc == 0 else vm.at[0]
             maps[rows, hh * BLOCK : (hh + 1) * BLOCK] = (served * used).astype(BF)
             here = (cell_row == i) & (cell_col == 2 * hh + cc)
@@ -406,6 +407,8 @@
     for hh in range(2):
         scales = serve(hh, 1, scales)
     ss_ref[0] = scales
+    store_served = pltpu.make_async_copy(served_now, sw_hbm.at[0], lsem.at[8])
+    store_served.start()
     for p in range(PARTS):
         for hh in range(2):
             qr[p, hh, mine] = qs[p, hh, rows16(tp), :]
@@ -565,6 +568,8 @@
                 both = jnp.concatenate([top[rows], low[rows]], axis=0)
                 dec[s, 0, :, first : first + HALF] = both.astype(BF)
 
+    store_served.wait()
+
     for copy in sent:
         copy.wait_send()
     each(lambda k: pick_copy(k).wait_send())
@@ -616,8 +621,9 @@
             jax.ShapeDtypeStruct((STEPS, 1, 16, D), BF),
         ),
         in_specs=[SM] * 5 + [HB] * 8,
-        out_specs=(VM, VM, VM),
+        out_specs=(HB, VM, VM),
         scratch_shapes=[
+            pltpu.VMEM((LAT, 512), BF),
             pltpu.VMEM((HEADS, 32, 256), BF),
             pltpu.VMEM((TP, 32, 256), BF),
             pltpu.VMEM((2, LAT, 256), BF),
@@ -646,7 +652,7 @@
             pltpu.VMEM((PARTS, YS, 128, 512), BF),
             pltpu.VMEM((CHUNKS, YS, 2, 16, HALF), BF),
             pltpu.VMEM((CHUNKS, YS, 2, 16, HALF), BF),
-            dma((8,)),
+            dma((9,)),
             dma((15,)),
             dma((REPS,)),
             dma((TP,)),

time: 101 us -> 101 us (level)
  no operation moved by 1% of the time
where the time goes in v6:
time: 101 us; the launch traced here: 99.7 us
  Pallas kernels  99 us (98%)
    pallas_call x1, Pallas kernels, local(): pl.pallas_call(everything, out_shape=(jax.ShapeDtypeStruct((1, LAT, 512),...  96.9 us
    pallas_call x1, Pallas kernels, local(): pl.pallas_call(hand_over, out_shape=tuple((jax.ShapeDtypeStruct(r.shape,...  2.16 us

profile of v6, /device:TPU:4, one launch (start us, length us, event | category | flops | bytes accessed | tf_op | source)
XLA Modules:
  0.0 99.7 jit_solution(6359716347402249103)
XLA Ops:
  0.6 96.9 %push_and_decode.1 = (bf16[1,512,512]{2,1,0:T(8,128)(2,1)}, f32[1,4,4]{2,1,0:T(4,128)}, bf16[2,1,16,7168]{3,2,1,0:T(8,128)(2,1)}) custom-call(s32[32]{0:T(128)} %slot_ref.1, s32[32]{0:T(128)} %bver_ref.1, s32[1,32]{1,0:T(1,128)} %rver_ref.1, f32[1,4,4]{2,1,0:T(4,128)} %oscale_ref.1, s32[1,16]{1,0:T(1,128)} %len_ref.1, bf16[2,32,256]{2,1,0:T(8,128)(2,1)} %tw_hbm.1, ...), custom_call_target="tpu_custom_call" | custom-call | tf_op jit(solution)/shard_map/push_and_decode/pallas_call | solution.py:616
  97.5 2.2 %hand_over.1 = (bf16[1,512,512]{2,1,0:T(8,128)(2,1)}, f32[1,4,4]{2,1,0:T(4,128)}, bf16[2,1,16,7168]{3,2,1,0:T(8,128)(2,1)}) custom-call(bf16[1,512,512]{2,1,0:T(8,128)(2,1)} %get-tuple-element.6.refs_0_, f32[1,4,4]{2,1,0:T(4,128)} %get-tuple-element.7.refs_1_, bf16[2,1,16,7168]{3,2,1,0:T(8,128)(2,1)} %get-tuple-element.8.refs_2_), custom_call_target="tpu_custom_call" | custom-call | tf_op jit(solution)/shard_map/hand_over/pallas_call | solution.py:700
